TPU v7x, 128 devices: a whole 4x4x4 slice. The times are simulated.
128 devices in a mesh: row: 8 (over y, core), col: 16 (over z, x).
Axes of the slice: x: 4, y: 4, z: 4, core: 2. Of those that a mesh axis runs over, the one named last changes fastest.
Arguments:
- children: float32 [12288, 6144], P('row', 'col'), may hold values from -6 to 6
- permutation: int32 [12288], replicated, may hold values from 0 to 12287, as said below
- type_counts: int32 [4], replicated, may hold values from 768 to 6144, as said below
- rotation: float32 [12288], replicated, may hold values from -3.140625 to 3.140625
- pole_values: float32 [12288], replicated, may hold values from -0.15 to 12287.15, as said below
- coupling: float32 [12288], replicated, may hold values from -3 to 3, as said below
- root_gap: int32 [4096], replicated, may hold values from 0 to 6142, as said below
- root_offset: float32 [4096], replicated, may hold values from 0.3 to 0.4
Outputs:
- merged: float32 [4096, 12288], P('col', 'row')
Inputs may be any that keep to these rules, and one draw needn't show every extreme that they name: A permutation of 0 to 12287. permutation[j] < 6144 for j < type_counts[0] + type_counts[1]; permutation[j] >= 6144 for type_counts[0] + type_counts[1] <= j < live; for every dense joint column j, the value permutation[j] + 6144 stands at some deflated position. The four counts sum to 12288; type_counts[1] lies in 768 to 1536; the smaller of type_counts[0] and type_counts[2] equals 1536; the larger of type_counts[0] + type_counts[1] and type_counts[1] + type_counts[2] equals 4608; type_counts[3] equals 6144. pole_values[j] lies within 0.15 of j. `coupling`: every entry has magnitude 0.3 or more. `root_gap`: distinct values.
All inputs are finite; a program needn't handle non-finite values.
Results may differ from a plain program's by a relative error of at most 0.00007.
Values sent between devices are 32-bit elements; how exact they have to be, the bound alone decides.
No kernel may reach another device: no remote copies, remote signals or barrier semaphores. Data moves between devices by JAX's collectives and lax.ppermute only.
A program may use at most 64 MiB of HBM per device.

v0:
```python
import math

import jax
import jax.numpy as jnp
from jax import lax
from jax.sharding import PartitionSpec as P

EPSILON = 1e-06
EXACT = lax.Precision.HIGHEST


def band_factors(type_counts, rotation, is_upper):
    order_size = rotation.shape[0]
    joint_index = jnp.arange(order_size, dtype=jnp.int32)
    upper_end = type_counts[0]
    dense_end = type_counts[0] + type_counts[1]
    live_count = dense_end + type_counts[2]
    paired = (joint_index >= upper_end) & (joint_index < dense_end)
    lower_only = (joint_index >= dense_end) & (joint_index < live_count)
    zero_fill = jnp.zeros_like(rotation)
    one_fill = jnp.ones_like(rotation)
    upper_part = jnp.where(
        joint_index < upper_end, one_fill, jnp.where(paired, jnp.cos(rotation), zero_fill)
    )
    bottom = jnp.where(paired, jnp.sin(rotation), jnp.where(lower_only, one_fill, zero_fill))
    return (jnp.where(is_upper, upper_part, bottom), live_count)


def invert_order(permutation):
    order_size = permutation.shape[0]
    joint_index = jnp.arange(order_size, dtype=jnp.int32)
    block_width = math.gcd(order_size, 512)
    targets = joint_index.reshape(order_size // block_width, block_width)

    def invert_one_block(target_block):
        hits = permutation[None, :] == target_block[:, None]
        return jnp.sum(
            jnp.where(hits, joint_index[None, :], jnp.zeros_like(joint_index)[None, :]), axis=1
        )

    return lax.map(invert_one_block, targets).reshape(order_size)


def side_vectors(columns, inverse, factor, coupling, pole_values, live_count):
    half_size = inverse.shape[0] // 2
    packed_sides = []
    for side_level in range(2):
        joint_rows = inverse[columns + side_level * half_size]
        live_mask = joint_rows < live_count
        numerator = jnp.where(live_mask, coupling[joint_rows], jnp.zeros_like(coupling[joint_rows]))
        packed_sides.append((pole_values[joint_rows], numerator, factor[joint_rows]))
    return lax.optimization_barrier(tuple(packed_sides))


def source_weights(packed_sides, base_part, offset, scale_part):
    weights = None
    for pole_side, numerator, factor_side in packed_sides:
        gap_diff = pole_side[:, None] - base_part[None, :] - offset[None, :]
        term = factor_side[:, None] * (numerator[:, None] / gap_diff)
        weights = term if weights is None else weights + term
    return weights * scale_part[None, :]


def norm_terms(
    first_joint, joint_share, coupling, pole_values, base_poles, root_offset, live_count
):
    joint_rows = first_joint + jnp.arange(joint_share, dtype=jnp.int32)
    pole_part = lax.dynamic_slice_in_dim(pole_values, first_joint, joint_share)
    coupling_part = lax.dynamic_slice_in_dim(coupling, first_joint, joint_share)
    numerator = jnp.where(joint_rows < live_count, coupling_part, jnp.zeros_like(coupling_part))
    root_count = base_poles.shape[0]
    block_width = math.gcd(root_count, 1024)

    def norm_one_block(packed_pair):
        gap_diff = pole_part[:, None] - packed_pair[0][None, :] - packed_pair[1][None, :]
        entries = numerator[:, None] / gap_diff
        return jnp.sum(entries * entries, axis=0)

    square_sums = lax.map(
        norm_one_block,
        (
            base_poles.reshape(root_count // block_width, block_width),
            root_offset.reshape(root_count // block_width, block_width),
        ),
    )
    return square_sums.reshape(root_count)


def per_device(
    children, permutation, type_counts, rotation, pole_values, coupling, root_gap, root_offset
):
    order_size = permutation.shape[0]
    half_size = order_size // 2
    groups = lax.axis_size("col")
    position = lax.axis_index("col")
    is_upper = lax.axis_index("row") < lax.axis_size("row") // 2
    inverse = invert_order(permutation)
    factor, live_count = band_factors(type_counts, rotation, is_upper)
    base_poles = pole_values[root_gap]
    root_count = root_gap.shape[0]
    joint_share = order_size // groups
    partial_norms = norm_terms(
        position * joint_share,
        joint_share,
        coupling,
        pole_values,
        base_poles,
        root_offset,
        live_count,
    )
    summed = lax.psum(partial_norms, "col")
    scale_all = lax.rsqrt(summed + EPSILON)
    blocks = lax.all_to_all(children, "col", split_axis=0, concat_axis=1, tiled=True)
    columns = jnp.arange(half_size, dtype=jnp.int32)
    packed_sides = side_vectors(columns, inverse, factor, coupling, pole_values, live_count)
    block_width = math.gcd(root_count, 256)

    def body_one_block(packed):
        weights = source_weights(packed_sides, packed[0], packed[1], packed[2])
        return lax.dot_general(
            weights,
            blocks,
            (((0,), (1,)), ((), ())),
            precision=EXACT,
            preferred_element_type=jnp.float32,
        )

    block_count = root_count // block_width
    stacked = lax.map(
        body_one_block,
        (
            base_poles.reshape(block_count, block_width),
            root_offset.reshape(block_count, block_width),
            scale_all.reshape(block_count, block_width),
        ),
    )
    results = stacked.reshape(root_count, blocks.shape[0])
    merged = lax.all_to_all(results, "col", split_axis=0, concat_axis=1, tiled=True)
    return merged


def solution(mesh):
    placed = (P("row", "col"), P(), P(), P(), P(), P(), P(), P())
    return jax.shard_map(
        per_device, mesh=mesh, in_specs=placed, out_specs=P("col", "row"), check_vma=False
    )
```

profile of v0, /device:TPU:0, one launch (start us, length us, event | category | flops | bytes accessed | tf_op | source)
XLA Modules:
  0.0 656.5 jit_solution(16496214650841588588)
XLA Ops:
  0.0 8.1 %all-to-all-start = ((f32[16,96,384]{2,1,0:T(8,128)}), f32[16,96,384]{2,1,0:T(8,128)S(1)}, u32[]{:S(2)}, u32[]{:S(2)}) async-start(f32[16,96,384]{2,1,0:T(8,128)} %bitcast.58), calls=%async_computation | async-start | bytes 4718592 | tf_op jit(solution)/shard_map/all_to_all | solution.py:113
  8.2 91.1 %while.33 = (s32[]{:T(128)}, s32[24,512]{1,0:T(8,128)S(1)}, s32[12288]{0:T(1024)S(1)}, s32[24,512]{1,0:T(8,128)S(1)}, s32[]{:T(128)}, /*index=5*/s32[]{:T(128)}) while((s32[]{:T(128)}, s32[24,512]{1,0:T(8,128)S(1)}, s32[12288]{0:T(1024)S(1)}, s32[24,512]{1,0:T(8,128)S(1)}, s32[]{:T(128)}, /*index=5*/s32[]{:T(128)}) %tuple.68), condition=%wide.region_6.7_spmd.clone, body=%wide.region_4.6_spmd.clone.sunk | while | flops 18873856 | bytes 61517 | solution.py:41
  8.2 3.7 fusion.41
  12.0 3.7 fusion.41
  23.4 3.7 fusion.41
  27.2 3.7 fusion.41
  31.0 3.7 fusion.41
  34.8 3.7 fusion.41
  38.6 3.7 fusion.41
  46.2 3.7 fusion.41
  50.0 3.7 fusion.41
  53.8 3.7 fusion.41
  57.6 3.7 fusion.41
  61.3 3.7 fusion.41
  68.9 3.7 fusion.41
  72.7 3.7 fusion.41
  76.5 3.7 fusion.41
  80.3 3.7 fusion.41
  84.1 3.7 fusion.41
  95.5 3.7 fusion.41
  99.3 34.3 %gather_fusion.4 = s32[6144]{0:T(1024)S(1)} fusion(s32[12288]{0:T(1024)S(1)} %bitcast.54, s32[6144]{0:T(1024)S(1)} %broadcast_clamp_fusion), kind=kCustom, calls=%fused_computation.4 | custom fusion | bytes 73728 | tf_op jit(solution)/shard_map/gather | solution.py:48
  133.7 34.3 %gather_fusion = s32[6144]{0:T(1024)S(1)} fusion(s32[12288]{0:T(1024)S(1)} %bitcast.55, s32[6144]{0:T(1024)S(1)} %iota_clamp_fusion), kind=kCustom, calls=%fused_computation | custom fusion | bytes 73728 | tf_op jit(solution)/shard_map/gather | solution.py:48
  168.7 34.3 %gather_fusion.6 = f32[6144]{0:T(1024)S(1)} fusion(f32[12288]{0:T(1024)S(1)} %copy-done.1, s32[6144]{0:T(1024)S(1)} %broadcast_clamp_fusion.1), kind=kCustom, calls=%fused_computation.6 | custom fusion | bytes 73728 | tf_op jit(solution)/shard_map/gather | solution.py:50
  203.1 34.3 %gather_fusion.2 = f32[6144]{0:T(1024)S(1)} fusion(f32[12288]{0:T(1024)S(1)} %copy-done.1, s32[6144]{0:T(1024)S(1)} %broadcast_clamp_fusion.2), kind=kCustom, calls=%fused_computation.2 | custom fusion | bytes 73728 | tf_op jit(solution)/shard_map/gather | solution.py:50
  240.7 34.3 %gather_fusion.7 = f32[6144]{0:T(1024)S(1)} fusion(f32[12288]{0:T(1024)S(1)} %select_select_fusion, s32[6144]{0:T(1024)S(1)} %broadcast_clamp_fusion.1), kind=kCustom, calls=%fused_computation.7 | custom fusion | bytes 73728 | tf_op jit(solution)/shard_map/gather | solution.py:51
  275.0 34.3 %gather_fusion.3 = f32[6144]{0:T(1024)S(1)} fusion(f32[12288]{0:T(1024)S(1)} %select_select_fusion, s32[6144]{0:T(1024)S(1)} %broadcast_clamp_fusion.2), kind=kCustom, calls=%fused_computation.3 | custom fusion | bytes 73728 | tf_op jit(solution)/shard_map/gather | solution.py:51
  309.3 34.3 %gather_fusion.5 = f32[6144]{0:T(1024)S(1)} fusion(f32[12288]{0:T(1024)S(1)} %copy-done, s32[6144]{0:T(1024)S(1)} %broadcast_clamp_fusion.1), kind=kCustom, calls=%fused_computation.5 | custom fusion | bytes 73728 | tf_op jit(solution)/shard_map/gather | solution.py:51
  343.6 34.3 %gather_fusion.1 = f32[6144]{0:T(1024)S(1)} fusion(f32[12288]{0:T(1024)S(1)} %copy-done, s32[6144]{0:T(1024)S(1)} %broadcast_clamp_fusion.2), kind=kCustom, calls=%fused_computation.1 | custom fusion | bytes 73728 | tf_op jit(solution)/shard_map/gather | solution.py:51
  378.1 23.0 %gather_fusion.8 = f32[4096]{0:T(1024)S(1)} fusion(f32[12288]{0:T(1024)S(1)} %copy-done, s32[4096]{0:T(1024)S(1)} %fusion.31), kind=kCustom, calls=%fused_computation.8 | custom fusion | bytes 49152 | tf_op jit(solution)/shard_map/gather | solution.py:99
  404.6 74.6 %psum.7 = f32[4096]{0:T(1024)S(1)} all-reduce(f32[4096]{0:T(1024)S(1)} %bitcast.68), channel_id=1, replica_groups=mesh['row'=8,'col'=16] {'col'}, use_global_device_ids=true, to_apply=%region_3.4 | all-reduce | flops 4096 | bytes 32768 | tf_op jit(solution)/shard_map/psum | solution.py:111
  480.9 154.5 %while.32 = (s32[]{:T(128)}, f32[16,256,96]{1,2,0:T(8,128)}, f32[6144]{0:T(1024)S(1)}, f32[6144]{0:T(1024)S(1)}, f32[6144]{0:T(1024)S(1)}, /*index=5*/f32[16,256...) while((s32[]{:T(128)}, f32[16,256,96]{1,2,0:T(8,128)}, ...), condition=%wide.region_8.9_spmd, body=%wide.region_7.8_spmd.sunk | while | flops 1827667968 | bytes 2614917 | solution.py:129
  480.9 9.6 %fusion.40 = f32[16,256,96]{1,2,0:T(8,128)} fusion(f32[16,256,96]{1,2,0:T(8,128)} %get-tuple-element.403, s32[]{:T(128)} %get-tuple-element.402, f32[96,6144]{1,0:T(8,128)} %get-tuple-element.426, f32[256]{0:T(256)S(1)} %bitcast.73, f32[6144]{0:T(1024)S(1)} %get-tuple-element.424, f32[6144]{0:T(1024)S(1)} %get-tuple-element.423, ...), kind=kOutput, calls=%fused_computation.34.clone.1 | convolution fusion | flops 1827667968 | bytes 2608640 | tf_op jit(solution)/shard_map/while/body/eval_jaxpr/dot_general | solution.py:120
  490.5 9.6 %fusion.40 = f32[16,256,96]{1,2,0:T(8,128)} fusion(f32[16,256,96]{1,2,0:T(8,128)} %get-tuple-element.403, s32[]{:T(128)} %get-tuple-element.402, f32[96,6144]{1,0:T(8,128)} %get-tuple-element.426, f32[256]{0:T(256)S(1)} %bitcast.73, f32[6144]{0:T(1024)S(1)} %get-tuple-element.424, f32[6144]{0:T(1024)S(1)} %get-tuple-element.423, ...), kind=kOutput, calls=%fused_computation.34.clone.1 | convolution fusion | flops 1827667968 | bytes 2608640 | tf_op jit(solution)/shard_map/while/body/eval_jaxpr/dot_general | solution.py:120
  500.2 9.6 %fusion.40 = f32[16,256,96]{1,2,0:T(8,128)} fusion(f32[16,256,96]{1,2,0:T(8,128)} %get-tuple-element.403, s32[]{:T(128)} %get-tuple-element.402, f32[96,6144]{1,0:T(8,128)} %get-tuple-element.426, f32[256]{0:T(256)S(1)} %bitcast.73, f32[6144]{0:T(1024)S(1)} %get-tuple-element.424, f32[6144]{0:T(1024)S(1)} %get-tuple-element.423, ...), kind=kOutput, calls=%fused_computation.34.clone.1 | convolution fusion | flops 1827667968 | bytes 2608640 | tf_op jit(solution)/shard_map/while/body/eval_jaxpr/dot_general | solution.py:120
  509.9 9.6 %fusion.40 = f32[16,256,96]{1,2,0:T(8,128)} fusion(f32[16,256,96]{1,2,0:T(8,128)} %get-tuple-element.403, s32[]{:T(128)} %get-tuple-element.402, f32[96,6144]{1,0:T(8,128)} %get-tuple-element.426, f32[256]{0:T(256)S(1)} %bitcast.73, f32[6144]{0:T(1024)S(1)} %get-tuple-element.424, f32[6144]{0:T(1024)S(1)} %get-tuple-element.423, ...), kind=kOutput, calls=%fused_computation.34.clone.1 | convolution fusion | flops 1827667968 | bytes 2608640 | tf_op jit(solution)/shard_map/while/body/eval_jaxpr/dot_general | solution.py:120
  519.5 9.6 %fusion.40 = f32[16,256,96]{1,2,0:T(8,128)} fusion(f32[16,256,96]{1,2,0:T(8,128)} %get-tuple-element.403, s32[]{:T(128)} %get-tuple-element.402, f32[96,6144]{1,0:T(8,128)} %get-tuple-element.426, f32[256]{0:T(256)S(1)} %bitcast.73, f32[6144]{0:T(1024)S(1)} %get-tuple-element.424, f32[6144]{0:T(1024)S(1)} %get-tuple-element.423, ...), kind=kOutput, calls=%fused_computation.34.clone.1 | convolution fusion | flops 1827667968 | bytes 2608640 | tf_op jit(solution)/shard_map/while/body/eval_jaxpr/dot_general | solution.py:120
  529.2 9.6 %fusion.40 = f32[16,256,96]{1,2,0:T(8,128)} fusion(f32[16,256,96]{1,2,0:T(8,128)} %get-tuple-element.403, s32[]{:T(128)} %get-tuple-element.402, f32[96,6144]{1,0:T(8,128)} %get-tuple-element.426, f32[256]{0:T(256)S(1)} %bitcast.73, f32[6144]{0:T(1024)S(1)} %get-tuple-element.424, f32[6144]{0:T(1024)S(1)} %get-tuple-element.423, ...), kind=kOutput, calls=%fused_computation.34.clone.1 | convolution fusion | flops 1827667968 | bytes 2608640 | tf_op jit(solution)/shard_map/while/body/eval_jaxpr/dot_general | solution.py:120
  538.8 9.6 %fusion.40 = f32[16,256,96]{1,2,0:T(8,128)} fusion(f32[16,256,96]{1,2,0:T(8,128)} %get-tuple-element.403, s32[]{:T(128)} %get-tuple-element.402, f32[96,6144]{1,0:T(8,128)} %get-tuple-element.426, f32[256]{0:T(256)S(1)} %bitcast.73, f32[6144]{0:T(1024)S(1)} %get-tuple-element.424, f32[6144]{0:T(1024)S(1)} %get-tuple-element.423, ...), kind=kOutput, calls=%fused_computation.34.clone.1 | convolution fusion | flops 1827667968 | bytes 2608640 | tf_op jit(solution)/shard_map/while/body/eval_jaxpr/dot_general | solution.py:120
  548.5 9.6 %fusion.40 = f32[16,256,96]{1,2,0:T(8,128)} fusion(f32[16,256,96]{1,2,0:T(8,128)} %get-tuple-element.403, s32[]{:T(128)} %get-tuple-element.402, f32[96,6144]{1,0:T(8,128)} %get-tuple-element.426, f32[256]{0:T(256)S(1)} %bitcast.73, f32[6144]{0:T(1024)S(1)} %get-tuple-element.424, f32[6144]{0:T(1024)S(1)} %get-tuple-element.423, ...), kind=kOutput, calls=%fused_computation.34.clone.1 | convolution fusion | flops 1827667968 | bytes 2608640 | tf_op jit(solution)/shard_map/while/body/eval_jaxpr/dot_general | solution.py:120
  558.2 9.6 %fusion.40 = f32[16,256,96]{1,2,0:T(8,128)} fusion(f32[16,256,96]{1,2,0:T(8,128)} %get-tuple-element.403, s32[]{:T(128)} %get-tuple-element.402, f32[96,6144]{1,0:T(8,128)} %get-tuple-element.426, f32[256]{0:T(256)S(1)} %bitcast.73, f32[6144]{0:T(1024)S(1)} %get-tuple-element.424, f32[6144]{0:T(1024)S(1)} %get-tuple-element.423, ...), kind=kOutput, calls=%fused_computation.34.clone.1 | convolution fusion | flops 1827667968 | bytes 2608640 | tf_op jit(solution)/shard_map/while/body/eval_jaxpr/dot_general | solution.py:120
  567.8 9.6 %fusion.40 = f32[16,256,96]{1,2,0:T(8,128)} fusion(f32[16,256,96]{1,2,0:T(8,128)} %get-tuple-element.403, s32[]{:T(128)} %get-tuple-element.402, f32[96,6144]{1,0:T(8,128)} %get-tuple-element.426, f32[256]{0:T(256)S(1)} %bitcast.73, f32[6144]{0:T(1024)S(1)} %get-tuple-element.424, f32[6144]{0:T(1024)S(1)} %get-tuple-element.423, ...), kind=kOutput, calls=%fused_computation.34.clone.1 | convolution fusion | flops 1827667968 | bytes 2608640 | tf_op jit(solution)/shard_map/while/body/eval_jaxpr/dot_general | solution.py:120
  577.5 9.6 %fusion.40 = f32[16,256,96]{1,2,0:T(8,128)} fusion(f32[16,256,96]{1,2,0:T(8,128)} %get-tuple-element.403, s32[]{:T(128)} %get-tuple-element.402, f32[96,6144]{1,0:T(8,128)} %get-tuple-element.426, f32[256]{0:T(256)S(1)} %bitcast.73, f32[6144]{0:T(1024)S(1)} %get-tuple-element.424, f32[6144]{0:T(1024)S(1)} %get-tuple-element.423, ...), kind=kOutput, calls=%fused_computation.34.clone.1 | convolution fusion | flops 1827667968 | bytes 2608640 | tf_op jit(solution)/shard_map/while/body/eval_jaxpr/dot_general | solution.py:120
  587.1 9.6 %fusion.40 = f32[16,256,96]{1,2,0:T(8,128)} fusion(f32[16,256,96]{1,2,0:T(8,128)} %get-tuple-element.403, s32[]{:T(128)} %get-tuple-element.402, f32[96,6144]{1,0:T(8,128)} %get-tuple-element.426, f32[256]{0:T(256)S(1)} %bitcast.73, f32[6144]{0:T(1024)S(1)} %get-tuple-element.424, f32[6144]{0:T(1024)S(1)} %get-tuple-element.423, ...), kind=kOutput, calls=%fused_computation.34.clone.1 | convolution fusion | flops 1827667968 | bytes 2608640 | tf_op jit(solution)/shard_map/while/body/eval_jaxpr/dot_general | solution.py:120
  596.8 9.6 %fusion.40 = f32[16,256,96]{1,2,0:T(8,128)} fusion(f32[16,256,96]{1,2,0:T(8,128)} %get-tuple-element.403, s32[]{:T(128)} %get-tuple-element.402, f32[96,6144]{1,0:T(8,128)} %get-tuple-element.426, f32[256]{0:T(256)S(1)} %bitcast.73, f32[6144]{0:T(1024)S(1)} %get-tuple-element.424, f32[6144]{0:T(1024)S(1)} %get-tuple-element.423, ...), kind=kOutput, calls=%fused_computation.34.clone.1 | convolution fusion | flops 1827667968 | bytes 2608640 | tf_op jit(solution)/shard_map/while/body/eval_jaxpr/dot_general | solution.py:120
  606.5 9.6 %fusion.40 = f32[16,256,96]{1,2,0:T(8,128)} fusion(f32[16,256,96]{1,2,0:T(8,128)} %get-tuple-element.403, s32[]{:T(128)} %get-tuple-element.402, f32[96,6144]{1,0:T(8,128)} %get-tuple-element.426, f32[256]{0:T(256)S(1)} %bitcast.73, f32[6144]{0:T(1024)S(1)} %get-tuple-element.424, f32[6144]{0:T(1024)S(1)} %get-tuple-element.423, ...), kind=kOutput, calls=%fused_computation.34.clone.1 | convolution fusion | flops 1827667968 | bytes 2608640 | tf_op jit(solution)/shard_map/while/body/eval_jaxpr/dot_general | solution.py:120
  616.1 9.6 %fusion.40 = f32[16,256,96]{1,2,0:T(8,128)} fusion(f32[16,256,96]{1,2,0:T(8,128)} %get-tuple-element.403, s32[]{:T(128)} %get-tuple-element.402, f32[96,6144]{1,0:T(8,128)} %get-tuple-element.426, f32[256]{0:T(256)S(1)} %bitcast.73, f32[6144]{0:T(1024)S(1)} %get-tuple-element.424, f32[6144]{0:T(1024)S(1)} %get-tuple-element.423, ...), kind=kOutput, calls=%fused_computation.34.clone.1 | convolution fusion | flops 1827667968 | bytes 2608640 | tf_op jit(solution)/shard_map/while/body/eval_jaxpr/dot_general | solution.py:120
  625.8 9.6 %fusion.40 = f32[16,256,96]{1,2,0:T(8,128)} fusion(f32[16,256,96]{1,2,0:T(8,128)} %get-tuple-element.403, s32[]{:T(128)} %get-tuple-element.402, f32[96,6144]{1,0:T(8,128)} %get-tuple-element.426, f32[256]{0:T(256)S(1)} %bitcast.73, f32[6144]{0:T(1024)S(1)} %get-tuple-element.424, f32[6144]{0:T(1024)S(1)} %get-tuple-element.423, ...), kind=kOutput, calls=%fused_computation.34.clone.1 | convolution fusion | flops 1827667968 | bytes 2608640 | tf_op jit(solution)/shard_map/while/body/eval_jaxpr/dot_general | solution.py:120
  635.4 19.5 %all_to_all.35 = f32[16,256,96]{1,2,0:T(8,128)S(1)} all-to-all(f32[16,256,96]{1,2,0:T(8,128)} %get-tuple-element.140), channel_id=1, replica_groups=mesh['row'=8,'col'=16] {'col'}, dimensions={0} | all-to-all | bytes 3145728 | tf_op jit(solution)/shard_map/all_to_all | solution.py:138
  (141 shorter events, 36.3 us)
Async XLA Ops:
  0.0 8.2 %copy-start.6 = (s32[12288]{0:T(1024)S(1)}, s32[12288]{0:T(1024)}, u32[]{:S(2)}) copy-start(s32[12288]{0:T(1024)} %param.15) | copy-start | bytes 147460
  0.0 479.2 %all-to-all-start = ((f32[16,96,384]{2,1,0:T(8,128)}), f32[16,96,384]{2,1,0:T(8,128)S(1)}, u32[]{:S(2)}, u32[]{:S(2)}) async-start(f32[16,96,384]{2,1,0:T(8,128)} %bitcast.58), calls=%async_computation | async-start | bytes 4718592 | tf_op jit(solution)/shard_map/all_to_all | solution.py:113
  167.9 0.8 copy-start.1
  203.0 34.3 %copy-start.5 = (s32[4]{0:T(128)S(1)}, s32[4]{0:T(128)}, u32[]{:S(2)}) copy-start(s32[4]{0:T(128)} %param.16) | copy-start | bytes 52
  203.0 36.9 %copy-start.3 = (f32[12288]{0:T(1024)S(1)}, f32[12288]{0:T(1024)}, u32[]{:S(2)}) copy-start(f32[12288]{0:T(1024)} %param.17) | copy-start | bytes 147460
  275.0 34.3 %copy-start = (f32[12288]{0:T(1024)S(1)}, f32[12288]{0:T(1024)}, u32[]{:S(2)}) copy-start(f32[12288]{0:T(1024)} %param.18) | copy-start | bytes 147460
  343.6 34.5 %copy-start.4 = (s32[4096]{0:T(1024)S(1)}, s32[4096]{0:T(1024)}, u32[]{:S(2)}) copy-start(s32[4096]{0:T(1024)} %param.20) | copy-start | bytes 49156
  378.1 23.1 %copy-start.2 = (f32[4096]{0:T(1024)S(1)}, f32[4096]{0:T(1024)}, u32[]{:S(2)}) copy-start(f32[4096]{0:T(1024)} %param.21) | copy-start | bytes 49156
where the time goes:
time: 657 us
  local copies, waits for them, and re-layouts  304 us (46%)
  matrix products  154 us (23%)
  blocking collectives  94.1 us (14%)
  other arithmetic  92.6 us (14%)
  starting transfers between devices  8.09 us (1%)
    dot_general x16, matrix products, body_one_block(): lax.dot_general(weights, blocks, (((0,), (1,)), ((), ())), precision=EXAC...  154 us
    reduce_sum x24, other arithmetic, invert_one_block(): jnp.sum(jnp.where(hits, joint_index[None, :], jnp.zeros_like(joint_index)...  88.7 us
    psum x1, blocking collectives, per_device(): summed = lax.psum(partial_norms, 'col')  74.6 us
    gather x2, local copies, waits for them, and re-layouts, side_vectors(): joint_rows = inverse[columns + side_level * half_size]  68.6 us
    gather x2, local copies, waits for them, and re-layouts, side_vectors(): factor[joint_rows]  68.6 us
    gather x2, local copies, waits for them, and re-layouts, side_vectors(): pole_values[joint_rows]  68.6 us
    gather x2, local copies, waits for them, and re-layouts, side_vectors(): coupling[joint_rows]  68.6 us
    gather x1, local copies, waits for them, and re-layouts, per_device(): base_poles = pole_values[root_gap]  23 us
  transfers between devices with their start and end apart: 1, of which 0 were waited for; matrix products, arithmetic and copies ran while one was open for 60% of the time, Pallas kernels for 0%

commit v1 on v0

v1 whole, which is shorter than its diff:
```python
import functools

import jax
import jax.numpy as jnp
from jax import lax
from jax.experimental import pallas as pl
from jax.experimental.pallas import tpu as pltpu
from jax.sharding import PartitionSpec as P

EPSILON = 1e-06
LANES = 128
CHUNK = 768
ROOT_TILE = 512
F32 = jnp.float32
BF16 = jnp.bfloat16


def product(left, right):
    return lax.dot_general(left, right, (((1,), (0,)), ((), ())), preferred_element_type=F32)


def product_lanes(left, right):
    return lax.dot_general(left, right, (((1,), (1,)), ((), ())), preferred_element_type=F32)


def split_two(value):
    high = value.astype(BF16)
    return high, (value - high.astype(F32)).astype(BF16)


def split_three(value):
    high = value.astype(BF16)
    rest = value - high.astype(F32)
    middle = rest.astype(BF16)
    return high, middle, (rest - middle.astype(F32)).astype(BF16)


def inverse_of(gap):
    first = pltpu.reciprocal(gap, approx=True)
    return first * (2.0 - gap * first)


def prep_kernel(
    source, used, amount, pole_row, coupling_row, table, gap_mine, gap_own, offset_own,
    column_scale, pole_wide, base_mine, root_scale,
):
    live = source.shape[1]
    groups = live // LANES
    place = source[...]
    high_place = place // LANES
    low_place = place - high_place * LANES
    row_hit = (
        lax.broadcasted_iota(jnp.int32, (groups, live), 0) == high_place
    ) & (used[...] > 0.0)
    low_hit = jnp.where(
        lax.broadcasted_iota(jnp.int32, (LANES, live), 0) == low_place, 1.0, 0.0
    ).astype(BF16)
    spread = []
    for values in (pole_row[...], amount[...]):
        total = None
        for piece in split_three(values):
            left = jnp.where(row_hit, piece.astype(F32), 0.0).astype(BF16)
            part = product_lanes(left, low_hit)
            total = part if total is None else total + part
        spread.append(total)
    column_scale[...] = spread[1]
    for group in range(groups):
        row = spread[0][group : group + 1, :]
        pole_wide[group * LANES : (group + 1) * LANES, :] = jnp.broadcast_to(
            row, (LANES, LANES)
        ).T

    def look_up(index_row):
        count = index_row.shape[1]
        high_index = index_row // LANES
        low_index = index_row - high_index * LANES
        hit = jnp.where(
            lax.broadcasted_iota(jnp.int32, (groups, count), 0) == high_index, 1.0, 0.0
        ).astype(BF16)
        total = None
        for piece in split_three(table[...]):
            part = product(piece, hit)
            total = part if total is None else total + part
        chosen = lax.broadcasted_iota(jnp.int32, (LANES, count), 0) == low_index
        return jnp.sum(jnp.where(chosen, total, 0.0), axis=0, keepdims=True)

    base_mine[...] = look_up(gap_mine[...])
    base_own = look_up(gap_own[...])
    for part in range(gap_own.shape[1] // LANES):
        lanes = slice(part * LANES, (part + 1) * LANES)
        base_tall = jnp.broadcast_to(base_own[:, lanes], (LANES, LANES)).T
        offset_tall = jnp.broadcast_to(offset_own[:, lanes], (LANES, LANES)).T
        total = jnp.zeros((LANES, LANES), F32)
        for group in range(groups):
            where = slice(group * LANES, (group + 1) * LANES)
            gap = (pole_row[:, where] - base_tall) - offset_tall
            entry = coupling_row[:, where] * inverse_of(gap)
            total = total + entry * entry
        root_scale[lanes, :] = lax.rsqrt(jnp.sum(total, axis=1, keepdims=True) + EPSILON)


def merge_kernel(
    mine, other, column_scale, pole_wide, base, offset, out_mine, out_other, pieces
):
    sources, band, width = mine.shape
    depth = sources * width
    roots = base.shape[1]
    per_source = width // LANES
    for source in range(sources):
        for part in range(per_source):
            lanes = slice(part * LANES, (part + 1) * LANES)
            at = slice(source * width + part * LANES, source * width + (part + 1) * LANES)
            row = source * per_source + part
            scale = column_scale[row : row + 1, :]
            for half, ref in enumerate((mine, other)):
                high, low = split_two(ref[source, :, lanes] * scale)
                pieces[half * band : (half + 1) * band, at] = high
                pieces[(2 + half) * band : (3 + half) * band, at] = low

    def one_tile(tile, carry):
        first = pl.multiple_of(tile * ROOT_TILE, ROOT_TILE)
        base_row = base[:, pl.ds(first, ROOT_TILE)]
        offset_row = offset[:, pl.ds(first, ROOT_TILE)]
        total = None
        for start in range(0, depth, CHUNK):
            poles = pole_wide[start : start + CHUNK, :]
            highs = []
            lows = []
            for part in range(ROOT_TILE // LANES):
                lanes = slice(part * LANES, (part + 1) * LANES)
                gap = (poles - base_row[:, lanes]) - offset_row[:, lanes]
                near = pltpu.reciprocal(gap, approx=True)
                high = near.astype(BF16)
                lows.append(((1.0 - gap * high.astype(F32)) * near).astype(BF16))
                highs.append(high)
            both = product(pieces[:, start : start + CHUNK], jnp.concatenate(highs, axis=1))
            rest = product(
                pieces[: 2 * band, start : start + CHUNK], jnp.concatenate(lows, axis=1)
            )
            part = both[: 2 * band] + both[2 * band :] + rest
            total = part if total is None else total + part
        for part in range(ROOT_TILE // LANES):
            lanes = slice(part * LANES, (part + 1) * LANES)
            block = tile * (ROOT_TILE // LANES) + part
            out_mine[block] = total[:band, lanes]
            out_other[block] = total[band:, lanes]
        return carry

    lax.fori_loop(0, roots // ROOT_TILE, one_tile, 0)


def finish_kernel(core, mine, other, root_scale, merged):
    sources, band, width = mine.shape
    for which, ref in ((core[0], mine), (1 - core[0], other)):
        rows = pl.ds(pl.multiple_of(which * width, width), width)
        scale = root_scale[rows, :]
        merged[rows, :] = ref[...].reshape(sources * band, width).T * scale


def vmem(count):
    return [pl.BlockSpec(memory_space=pltpu.VMEM)] * count


def per_device(
    children, permutation, type_counts, rotation, pole_values, coupling, root_gap, root_offset
):
    order_size = permutation.shape[0]
    half_size = order_size // 2
    groups = lax.axis_size("col")
    position = lax.axis_index("col")
    row_index = lax.axis_index("row")
    rows = lax.axis_size("row")
    core = row_index % 2
    is_upper = row_index < rows // 2
    root_count = root_gap.shape[0]
    share = root_count // groups
    band = children.shape[0] // groups
    width = children.shape[1]
    pairs = [(index, index ^ 1) for index in range(rows)]

    received = lax.all_to_all(
        children.reshape(groups, band, width), "col", split_axis=0, concat_axis=0, tiled=True
    )

    joint_index = jnp.arange(half_size, dtype=jnp.int32)
    upper_end = type_counts[0]
    dense_end = type_counts[0] + type_counts[1]
    live_count = dense_end + type_counts[2]
    paired = (joint_index >= upper_end) & (joint_index < dense_end)
    lower_only = (joint_index >= dense_end) & (joint_index < live_count)
    angle = rotation[:half_size]
    upper_part = jnp.where(joint_index < upper_end, 1.0, jnp.where(paired, jnp.cos(angle), 0.0))
    lower_part = jnp.where(paired, jnp.sin(angle), jnp.where(lower_only, 1.0, 0.0))
    factor = jnp.where(is_upper, upper_part, lower_part)
    used = jnp.where(
        jnp.where(is_upper, joint_index < dense_end, paired | lower_only), 1.0, 0.0
    )
    live_coupling = jnp.where(joint_index < live_count, coupling[:half_size], 0.0)
    order = permutation[:half_size]
    source = jnp.where(order >= half_size, order - half_size, order)
    poles = pole_values[:half_size]
    gap_blocks = root_gap.reshape(groups, 2, share // 2)
    offset_blocks = root_offset.reshape(groups, 2, share // 2)
    gap_mine = lax.dynamic_index_in_dim(gap_blocks, core, 1, keepdims=False).reshape(1, -1)
    offset_mine = lax.dynamic_index_in_dim(offset_blocks, core, 1, keepdims=False).reshape(1, -1)
    gap_own = lax.dynamic_slice_in_dim(root_gap, position * share, share).reshape(1, -1)
    offset_own = lax.dynamic_slice_in_dim(root_offset, position * share, share).reshape(1, -1)

    column_scale, pole_wide, base_mine, root_scale = pl.pallas_call(
        prep_kernel,
        out_shape=(
            jax.ShapeDtypeStruct((half_size // LANES, LANES), F32),
            jax.ShapeDtypeStruct((half_size, LANES), F32),
            jax.ShapeDtypeStruct((1, root_count // 2), F32),
            jax.ShapeDtypeStruct((share, 1), F32),
        ),
        in_specs=vmem(9),
        out_specs=tuple(vmem(4)),
        compiler_params=pltpu.CompilerParams(vmem_limit_bytes=40 * 2**20),
        cost_estimate=pl.CostEstimate(
            flops=2 * 10**9, bytes_accessed=4 * 10**6, transcendentals=2 * 10**6
        ),
    )(
        source.reshape(1, -1),
        used.reshape(1, -1),
        (live_coupling * factor).reshape(1, -1),
        poles.reshape(1, -1),
        live_coupling.reshape(1, -1),
        poles.reshape(-1, LANES).T,
        gap_mine,
        gap_own,
        offset_own,
    )

    swapped = lax.ppermute(received, "row", pairs)
    piece = jax.ShapeDtypeStruct((groups, band, share // 2), F32)
    out_mine, out_other = pl.pallas_call(
        merge_kernel,
        out_shape=(piece, piece),
        in_specs=vmem(6),
        out_specs=tuple(vmem(2)),
        scratch_shapes=[pltpu.VMEM((4 * band, groups * width), BF16)],
        compiler_params=pltpu.CompilerParams(vmem_limit_bytes=48 * 2**20),
        cost_estimate=pl.CostEstimate(
            flops=30 * 10**9, bytes_accessed=10 * 10**6, transcendentals=12 * 10**6
        ),
    )(received, swapped, column_scale, pole_wide, base_mine, offset_mine)

    def exchange(value):
        return lax.all_to_all(value, "col", split_axis=0, concat_axis=0, tiled=True)

    done_mine = exchange(out_mine)
    done_other = exchange(lax.ppermute(out_other, "row", pairs))
    return pl.pallas_call(
        finish_kernel,
        out_shape=jax.ShapeDtypeStruct((share, groups * band), F32),
        in_specs=[pl.BlockSpec(memory_space=pltpu.SMEM)] + vmem(3),
        out_specs=pl.BlockSpec(memory_space=pltpu.VMEM),
        compiler_params=pltpu.CompilerParams(vmem_limit_bytes=32 * 2**20),
    )(core.reshape(1), done_mine, done_other, root_scale)


def solution(mesh):
    placed = (P("row", "col"), P(), P(), P(), P(), P(), P(), P())
    return jax.shard_map(
        per_device, mesh=mesh, in_specs=placed, out_specs=P("col", "row"), check_vma=False
    )
```

time: 657 us -> 111 us (0.17)
  local copies, waits for them, and re-layouts: 304 us -> 2.59 us
  matrix products: 154 us -> 0 us
  other arithmetic: 92.6 us -> 1.47 us
  Pallas kernels: 0 us -> 30.1 us
  blocking collectives: 94.1 us -> 73.5 us
  starting transfers between devices: 8.09 us -> 0.58 us
    gather x9 -> x0, local copies, waits for them, and re-layouts: 297 us -> none  [the longest x2 68.6 us: side_vectors(): joint_rows = inverse[columns + side_level * half_size]]
    dot_general x16 -> x0, matrix products: 154 us -> none  [body_one_block(): lax.dot_general(weights, blocks, (((0,), (1,)), ((), ())), precision=EXAC...]
    reduce_sum x28 -> x0, other arithmetic: 91.6 us -> none  [the longest x24 88.7 us: invert_one_block(): jnp.sum(jnp.where(hits, joint_index[None, :], jnp.zeros_like(joint_index)...]
    psum x1 -> x0, blocking collectives: 74.6 us -> none  [per_device(): summed = lax.psum(partial_norms, 'col')]
    all_to_all x1 -> x3, blocking collectives: 19.5 us -> 73.5 us  [the longest x1 39.3 us: per_device(): lax.all_to_all(children.reshape(groups, band, width), 'col', split_axis=0...]
    pallas_call x0 -> x3, Pallas kernels: none -> 30.1 us  [the longest x1 22.3 us: per_device(): pl.pallas_call(merge_kernel, out_shape=(piece, piece), in_specs=vmem(6),...]
    all_to_all x1 -> x0, starting transfers between devices: 8.09 us -> none  [per_device(): lax.all_to_all(children, 'col', split_axis=0, concat_axis=1, tiled=True)]
  transfers between devices with their start and end apart: 1 -> 2, of which waited for: 0 -> 0; matrix products, arithmetic and copies ran while one was open for 60% -> 2% of each run, Pallas kernels for 0% -> 6%
where the time goes in v1:
time: 111 us; the launch traced here: 110 us
  blocking collectives  73.5 us (66%)
  Pallas kernels  30.1 us (27%)
  local copies, waits for them, and re-layouts  2.59 us (2%)
  between operations  2.02 us (2%)
  other arithmetic  1.47 us (1%)
    all_to_all x1, blocking collectives, per_device(): lax.all_to_all(children.reshape(groups, band, width), 'col', split_axis=0...  39.3 us
    all_to_all x2, blocking collectives, exchange(): return lax.all_to_all(value, 'col', split_axis=0, concat_axis=0, tiled=True)  34.1 us
    pallas_call x1, Pallas kernels, per_device(): pl.pallas_call(merge_kernel, out_shape=(piece, piece), in_specs=vmem(6),...  22.3 us
    pallas_call x1, Pallas kernels, per_device(): pl.pallas_call(prep_kernel, out_shape=(jax.ShapeDtypeStruct((half_size //...  6.07 us
  transfers between devices with their start and end apart: 2, of which 0 were waited for; matrix products, arithmetic and copies ran while one was open for 2% of the time, Pallas kernels for 6%

profile of v1, /device:TPU:0, one launch (start us, length us, event | category | flops | bytes accessed | tf_op | source)
XLA Modules:
  0.0 110.2 jit_solution(2860033508279758613)
XLA Ops:
  0.0 0.0 copy-start.5
  0.0 0.0 copy-start.6
  0.0 0.0 copy-start.2
  0.0 0.0 copy-start.7
  0.0 0.0 copy-start.1
  0.0 0.0 copy-start.3
  0.0 0.0 copy-start.4
  0.0 39.3 %all_to_all.15.mine = f32[16,96,384]{2,1,0:T(8,128)S(1)} all-to-all(f32[16,96,384]{2,1,0:T(8,128)} %bitcast.27), channel_id=1, replica_groups=mesh['row'=8,'col'=16] {'col'}, dimensions={0} | all-to-all | bytes 4718592 | tf_op jit(solution)/shard_map/all_to_all | solution.py:181
  39.3 0.0 collective-permute-start
  39.4 0.0 copy-done.5
  39.4 0.1 dynamic_slice.15
  39.4 0.0 copy-done.6
  39.4 0.1 dynamic_slice.16
  39.5 0.0 copy-done.2
  39.5 0.1 copy.9
  39.6 0.0 copy-done.7
  39.6 0.6 fusion.2
  42.2 0.0 copy-done.1
  42.2 0.0 copy-done.3
  42.2 0.0 copy-done.4
  42.2 0.7 slice_select_fusion
  43.0 0.7 select_select_fusion.used
  43.7 6.1 %shard_map.82 = (f32[48,128]{1,0:T(8,128)S(1)}, f32[6144,128]{1,0:T(8,128)S(1)}, f32[1,2048]{1,0:T(1,128)S(1)}, f32[256,1]{1,0:T(8,128)S(1)}) custom-call(s32[1,6144]{1,0:T(1,128)S(1)} %bitcast.21, f32[1,6144]{1,0:T(1,128)S(1)} %select_select_fusion.used, f32[1,6144]{1,0:T(1,128)S(1)} %bitcast.24, f32[1,6144]{1,0:T(1,128)S(1)} %bitcast.22, ...), custom_call_target="tpu_custom_call" | custom-call | flops 2000000000 | bytes 4000000 | tf_op jit(solution)/shard_map/pallas_call | solution.py:209
  49.8 0.0 copy-start
  49.8 1.6 %copy-done = f32[6144,128]{1,0:T(8,128)} copy-done((f32[6144,128]{1,0:T(8,128)}, f32[6144,128]{1,0:T(8,128)S(1)}, u32[]{:S(2)}) %copy-start) | copy-done | bytes 3145752
  51.5 0.0 collective-permute-done.other
  51.5 22.3 %shard_map.83 = (f32[16,96,128]{2,1,0:T(8,128)S(1)}, f32[16,96,128]{2,1,0:T(8,128)S(1)}) custom-call(f32[16,96,384]{2,1,0:T(8,128)S(1)} %all_to_all.15.mine, f32[16,96,384]{2,1,0:T(8,128)} %collective-permute-done.other, f32[48,128]{1,0:T(8,128)S(1)} %get-tuple-element.11.column_scale, f32[6144,128]{1,0:T(8,128)} %copy-done, ...), custom_call_target="tpu_custom_call" | custom-call | flops 30000001024 | bytes 10000000 | tf_op jit(solution)/shard_map/pallas_call | solution.py:237
  73.8 0.6 collective-permute-start.1
  74.4 17.4 %all_to_all.16.mine = f32[16,96,128]{2,1,0:T(8,128)S(1)} all-to-all(f32[16,96,128]{2,1,0:T(8,128)S(1)} %get-tuple-element.14), channel_id=1, replica_groups=mesh['row'=8,'col'=16] {'col'}, dimensions={0} | all-to-all | bytes 1572864 | tf_op jit(solution)/shard_map/all_to_all | solution.py:250
  91.8 0.0 collective-permute-done.1
  91.8 16.7 %all_to_all.17.other = f32[16,96,128]{2,1,0:T(8,128)S(1)} all-to-all(f32[16,96,128]{2,1,0:T(8,128)S(1)} %collective-permute-done.1), channel_id=1, replica_groups=mesh['row'=8,'col'=16] {'col'}, dimensions={0} | all-to-all | bytes 1572864 | tf_op jit(solution)/shard_map/all_to_all | solution.py:250
  108.5 1.7 %shard_map.84 = f32[256,1536]{1,0:T(8,128)} custom-call(s32[1]{0:T(128)} %bitcast.core, f32[16,96,128]{2,1,0:T(8,128)S(1)} %all_to_all.16.mine, f32[16,96,128]{2,1,0:T(8,128)S(1)} %all_to_all.17.other, f32[256,1]{1,0:T(8,128)S(1)} %get-tuple-element.16.root_scale), custom_call_target="tpu_custom_call" | custom-call | tf_op jit(solution)/shard_map/pallas_call | solution.py:254
  (4 shorter events, 0.0 us)
Async XLA Ops:
  0.0 39.4 %copy-start.5 = (s32[4096]{0:T(1024)S(1)}, s32[4096]{0:T(1024)}, u32[]{:S(2)}) copy-start(s32[4096]{0:T(1024)} %param.14) | copy-start | bytes 49156
  0.0 39.4 %copy-start.6 = (f32[4096]{0:T(1024)S(1)}, f32[4096]{0:T(1024)}, u32[]{:S(2)}) copy-start(f32[4096]{0:T(1024)} %param.15) | copy-start | bytes 49156
  0.0 39.5 %copy-start.2 = (f32[12288]{0:T(1024)S(1)}, f32[12288]{0:T(1024)}, u32[]{:S(2)}) copy-start(f32[12288]{0:T(1024)} %param.12) | copy-start | bytes 147460
  0.0 39.6 %copy-start.7 = (s32[4]{0:T(128)S(1)}, s32[4]{0:T(128)}, u32[]{:S(2)}) copy-start(s32[4]{0:T(128)} %param.10) | copy-start | bytes 52
  0.0 42.2 %copy-start.1 = (s32[12288]{0:T(1024)S(1)}, s32[12288]{0:T(1024)}, u32[]{:S(2)}) copy-start(s32[12288]{0:T(1024)} %param.9) | copy-start | bytes 147460
  0.0 42.2 %copy-start.3 = (f32[12288]{0:T(1024)S(1)}, f32[12288]{0:T(1024)}, u32[]{:S(2)}) copy-start(f32[12288]{0:T(1024)} %param.13) | copy-start | bytes 147460
  0.0 42.2 %copy-start.4 = (f32[12288]{0:T(1024)S(1)}, f32[12288]{0:T(1024)}, u32[]{:S(2)}) copy-start(f32[12288]{0:T(1024)} %param.11) | copy-start | bytes 147460
  39.3 12.1 %collective-permute-start = (f32[16,96,384]{2,1,0:T(8,128)S(1)}, f32[16,96,384]{2,1,0:T(8,128)}, u32[]{:S(2)}, u32[]{:S(2)}) collective-permute-start(f32[16,96,384]{2,1,0:T(8,128)S(1)} %all_to_all.15.mine), channel_id=1, source_target_pairs={{0,16},{16,0},{32,48},{48,32},{64,80},{80,64},{96,112},{112,96},{1... | collective-permute-start | bytes 7077896 | tf_op jit(solution)/shard_map/ppermute | solution.py:235
  49.8 1.6 %copy-start = (f32[6144,128]{1,0:T(8,128)}, f32[6144,128]{1,0:T(8,128)S(1)}, u32[]{:S(2)}) copy-start(f32[6144,128]{1,0:T(8,128)S(1)} %get-tuple-element.12.pole_wide) | copy-start | bytes 9437188
  73.8 18.0 %collective-permute-start.1 = (f32[16,96,128]{2,1,0:T(8,128)S(1)}, f32[16,96,128]{2,1,0:T(8,128)S(1)}, u32[]{:S(2)}, u32[]{:S(2)}) collective-permute-start(f32[16,96,128]{2,1,0:T(8,128)S(1)} %get-tuple-element.15), channel_id=1, source_target_pairs={{0,16},{16,0},{32,48},{48,32},{64,80},{80,64},{96,112},{112,96},{1... | collective-permute-start | bytes 2359304 | tf_op jit(solution)/shard_map/ppermute | solution.py:253

commit v2 on v1

v2 whole, which is shorter than its diff:
```python
import functools

import jax
import jax.numpy as jnp
from jax import lax
from jax.experimental import pallas as pl
from jax.experimental.pallas import tpu as pltpu
from jax.sharding import PartitionSpec as P

EPSILON = 1e-06
LANES = 128
CHUNK = 1024
ROOT_TILE = 512
F32 = jnp.float32
BF16 = jnp.bfloat16


def product(left, right):
    return lax.dot_general(left, right, (((1,), (0,)), ((), ())), preferred_element_type=F32)


def product_lanes(left, right):
    return lax.dot_general(left, right, (((1,), (1,)), ((), ())), preferred_element_type=F32)


def split_two(value):
    high = value.astype(BF16)
    return high, (value - high.astype(F32)).astype(BF16)


def split_three(value):
    high = value.astype(BF16)
    rest = value - high.astype(F32)
    middle = rest.astype(BF16)
    return high, middle, (rest - middle.astype(F32)).astype(BF16)


def inverse_of(gap):
    first = pltpu.reciprocal(gap, approx=True)
    return first * (2.0 - gap * first)


def prep_kernel(
    counts, core, position, row_index, rows_total, permutation, rotation, pole_values, coupling,
    root_gap, root_offset, column_scale, pole_wide, rows, root_scale, gap_mine, table,
):
    live = permutation.shape[1] // 2
    share = root_scale.shape[0]
    blocks = root_gap.shape[1] // share
    joint = lax.broadcasted_iota(jnp.int32, (1, live), 1)
    upper_end = counts[0]
    dense_end = upper_end + counts[1]
    live_count = dense_end + counts[2]
    paired = (joint >= upper_end) & (joint < dense_end)
    lower_only = (joint >= dense_end) & (joint < live_count)
    angle = rotation[:, :live]
    upper_part = jnp.where(joint < upper_end, 1.0, jnp.where(paired, jnp.cos(angle), 0.0))
    lower_part = jnp.where(paired, jnp.sin(angle), jnp.where(lower_only, 1.0, 0.0))
    upper_used = jnp.where(joint < dense_end, 1.0, 0.0)
    lower_used = jnp.where(paired | lower_only, 1.0, 0.0)
    is_upper = row_index[0] < rows_total[0] // 2
    factor = jnp.where(is_upper, upper_part, lower_part)
    used = jnp.where(is_upper, upper_used, lower_used)
    coupling_row = jnp.where(joint < live_count, coupling[:, :live], 0.0)
    pole_row = pole_values[:, :live]
    order = permutation[:, :live]
    place = jnp.where(order >= live, order - live, order)
    groups = live // LANES
    high_place = place // LANES
    low_place = place - high_place * LANES
    row_hit = (
        lax.broadcasted_iota(jnp.int32, (groups, live), 0) == high_place
    ) & (used > 0.0)
    low_hit = jnp.where(
        lax.broadcasted_iota(jnp.int32, (LANES, live), 0) == low_place, 1.0, 0.0
    ).astype(BF16)
    pieces = [
        jnp.where(row_hit, piece.astype(F32), 0.0).astype(BF16)
        for values in (pole_row, coupling_row * factor)
        for piece in split_three(values)
    ]
    spread = product_lanes(jnp.concatenate(pieces, axis=0), low_hit)
    placed = [
        (spread[first : first + groups] + spread[first + groups : first + 2 * groups])
        + spread[first + 2 * groups : first + 3 * groups]
        for first in (0, 3 * groups)
    ]
    column_scale[...] = placed[1]
    for group in range(groups):
        pole_wide[group * LANES : (group + 1) * LANES, :] = jnp.broadcast_to(
            placed[0][group : group + 1, :], (LANES, LANES)
        ).T
    table[...] = jnp.zeros_like(table)
    for group in range(groups):
        table[group : group + 1, :] = pole_row[:, group * LANES : (group + 1) * LANES]
    table_pieces = split_three(table[...].T)

    def look_up(index_row):
        count = index_row.shape[1]
        high_index = index_row // LANES
        low_index = index_row - high_index * LANES
        hit = jnp.where(
            lax.broadcasted_iota(jnp.int32, (LANES, count), 0) == high_index, 1.0, 0.0
        ).astype(BF16)
        total = None
        for piece in table_pieces:
            part = product(piece, hit)
            total = part if total is None else total + part
        chosen = lax.broadcasted_iota(jnp.int32, (LANES, count), 0) == low_index
        return jnp.sum(jnp.where(chosen, total, 0.0), axis=0, keepdims=True)

    half_share = share // 2
    for block in range(blocks):
        lanes = pl.ds(pl.multiple_of(block * share + core[0] * half_share, LANES), half_share)
        here = slice(block * half_share, (block + 1) * half_share)
        gap_mine[:, here] = root_gap[:, lanes]
        rows[1:2, here] = root_offset[:, lanes]
    rows[0:1, :] = look_up(gap_mine[...])
    own = pl.ds(pl.multiple_of(position[0] * share, LANES), share)
    base_own = look_up(root_gap[:, own])
    offset_own = root_offset[:, own]
    for part in range(share // LANES):
        lanes = slice(part * LANES, (part + 1) * LANES)
        base_tall = jnp.broadcast_to(base_own[:, lanes], (LANES, LANES)).T
        offset_tall = jnp.broadcast_to(offset_own[:, lanes], (LANES, LANES)).T
        total = jnp.zeros((LANES, LANES), F32)
        for group in range(groups):
            where = slice(group * LANES, (group + 1) * LANES)
            gap = (pole_row[:, where] - base_tall) - offset_tall
            entry = coupling_row[:, where] * inverse_of(gap)
            total = total + entry * entry
        root_scale[lanes, :] = lax.rsqrt(jnp.sum(total, axis=1, keepdims=True) + EPSILON)


def merge_kernel(core, mine, other, column_scale, pole_wide, rows, out, pieces):
    groups, band, width = mine.shape
    parts = width // LANES
    depth = groups * width
    tiles = rows.shape[1] // ROOT_TILE
    per_tile = ROOT_TILE // LANES
    for half, ref in enumerate((mine, other)):
        for source in range(groups):
            for part in range(parts):
                lanes = slice(part * LANES, (part + 1) * LANES)
                first = source * width + part * LANES
                at = slice(first, first + LANES)
                row = source * parts + part
                high, low = split_two(ref[source, :, lanes] * column_scale[row : row + 1, :])
                pieces[half * band : (half + 1) * band, at] = high
                pieces[(2 + half) * band : (3 + half) * band, at] = low

    def one_tile(tile, carry):
        first = pl.multiple_of(tile * ROOT_TILE, ROOT_TILE)
        base_row = rows[0:1, pl.ds(first, ROOT_TILE)]
        offset_row = rows[1:2, pl.ds(first, ROOT_TILE)]
        total = None
        for start in range(0, depth, CHUNK):
            column = pole_wide[start : start + CHUNK, :]
            highs = []
            lows = []
            for part in range(per_tile):
                lanes = slice(part * LANES, (part + 1) * LANES)
                gap = (column - base_row[:, lanes]) - offset_row[:, lanes]
                high = pltpu.reciprocal(gap, approx=True).astype(BF16)
                lows.append((1.0 - gap * high.astype(F32)).astype(BF16) * high)
                highs.append(high)
            both = product(pieces[:, start : start + CHUNK], jnp.concatenate(highs, axis=1))
            rest = product(
                pieces[: 2 * band, start : start + CHUNK], jnp.concatenate(lows, axis=1)
            )
            part = both[: 2 * band] + both[2 * band :] + rest
            total = part if total is None else total + part
        for half, which in enumerate((core[0], 1 - core[0])):
            for part in range(per_tile):
                lanes = slice(part * LANES, (part + 1) * LANES)
                block = which * groups + tile * per_tile + part
                out[block] = total[half * band : (half + 1) * band, lanes]
        return carry

    lax.fori_loop(0, tiles, one_tile, 0)


def finish_kernel(blocks, root_scale, merged, made, sems):
    sources, band, width = blocks.shape
    groups = sources // 2
    copies = []
    for half in range(2):
        rows = pl.ds(half * width, width)
        tall = blocks[half * groups : (half + 1) * groups].reshape(groups * band, width)
        made[rows, :] = tall.T * root_scale[rows, :]
        copies.append(pltpu.make_async_copy(made.at[rows], merged.at[rows], sems.at[half]))
        copies[half].start()
    for copy in copies:
        copy.wait()


def hbm(count):
    return [pl.BlockSpec(memory_space=pltpu.HBM)] * count


def vmem(count):
    return [pl.BlockSpec(memory_space=pltpu.VMEM)] * count


def per_device(
    children, permutation, type_counts, rotation, pole_values, coupling, root_gap, root_offset
):
    order_size = permutation.shape[0]
    half_size = order_size // 2
    groups = lax.axis_size("col")
    position = lax.axis_index("col")
    row_index = lax.axis_index("row")
    rows = lax.axis_size("row")
    core = row_index % 2
    is_upper = row_index < rows // 2
    root_count = root_gap.shape[0]
    share = root_count // groups
    band = children.shape[0] // groups
    width = children.shape[1]
    pairs = [(index, index ^ 1) for index in range(rows)]

    mine = lax.all_to_all(
        children.reshape(groups, band, width), "col", split_axis=0, concat_axis=0, tiled=True
    )
    mine, permutation = lax.optimization_barrier((mine, permutation))
    other = lax.ppermute(mine, "row", pairs)
    column_scale, pole_wide, root_rows, root_scale = pl.pallas_call(
        prep_kernel,
        out_shape=(
            jax.ShapeDtypeStruct((half_size // LANES, LANES), F32),
            jax.ShapeDtypeStruct((half_size, LANES), F32),
            jax.ShapeDtypeStruct((2, root_count // 2), F32),
            jax.ShapeDtypeStruct((share, 1), F32),
        ),
        in_specs=[pl.BlockSpec(memory_space=pltpu.SMEM)] * 5 + vmem(6),
        out_specs=tuple(vmem(4)),
        scratch_shapes=[
            pltpu.VMEM((1, root_count // 2), jnp.int32),
            pltpu.VMEM((LANES, LANES), F32),
        ],
        compiler_params=pltpu.CompilerParams(vmem_limit_bytes=32 * 2**20),
        cost_estimate=pl.CostEstimate(
            flops=4 * 10**9, bytes_accessed=4 * 10**6, transcendentals=2 * 10**6
        ),
    )(
        type_counts,
        core.reshape(1),
        position.reshape(1),
        row_index.reshape(1),
        jnp.full((1,), rows, jnp.int32),
        *(
            value.reshape(1, -1)
            for value in (permutation, rotation, pole_values, coupling, root_gap, root_offset)
        ),
    )
    blocks = pl.pallas_call(
        merge_kernel,
        out_shape=jax.ShapeDtypeStruct((2 * groups, band, share // 2), F32),
        in_specs=[pl.BlockSpec(memory_space=pltpu.SMEM)] + vmem(5),
        out_specs=vmem(1)[0],
        scratch_shapes=[pltpu.VMEM((4 * band, groups * width), BF16)],
        compiler_params=pltpu.CompilerParams(vmem_limit_bytes=32 * 2**20),
        cost_estimate=pl.CostEstimate(
            flops=30 * 10**9, bytes_accessed=10 * 10**6, transcendentals=12 * 10**6
        ),
    )(core.reshape(1), mine, other, column_scale, pole_wide, root_rows)
    chips = [
        [(pair * 2 + half) * groups + index for half in range(2) for index in range(groups)]
        for pair in range(rows // 2)
    ]
    blocks = lax.all_to_all(
        blocks, ("row", "col"), split_axis=0, concat_axis=0, axis_index_groups=chips, tiled=True
    )
    return pl.pallas_call(
        finish_kernel,
        out_shape=jax.ShapeDtypeStruct((share, groups * band), F32),
        in_specs=vmem(2),
        out_specs=hbm(1)[0],
        scratch_shapes=[
            pltpu.VMEM((share, groups * band), F32),
            pltpu.SemaphoreType.DMA((2,)),
        ],
        compiler_params=pltpu.CompilerParams(vmem_limit_bytes=16 * 2**20),
    )(blocks, root_scale)


def solution(mesh):
    placed = (P("row", "col"), P(), P(), P(), P(), P(), P(), P())
    return jax.shard_map(
        per_device, mesh=mesh, in_specs=placed, out_specs=P("col", "row"), check_vma=False
    )
```

time: 111 us -> 93.1 us (0.84)
  blocking collectives: 73.5 us -> 65.8 us
  Pallas kernels: 30.1 us -> 26.6 us
  local copies, waits for them, and re-layouts: 2.59 us -> 0.03 us
  between operations: 2.02 us -> 0.08 us
  other arithmetic: 1.47 us -> 0 us
    all_to_all x2 -> x1, blocking collectives: 34.1 us -> 26.5 us  [per_device(): lax.all_to_all(blocks, ('row', 'col'), split_axis=0, concat_axis=0, axis_...]
    pallas_call x1, Pallas kernels: 22.3 us -> 19.8 us  [per_device(): pl.pallas_call(merge_kernel, out_shape=jax.ShapeDtypeStruct((2 * groups,...]
    unnamed x16 -> x14, local copies, waits for them, and re-layouts: 1.67 us -> 0.03 us
    select_n x3 -> x0, other arithmetic: 1.47 us -> none  [the longest x1 0.74 us: per_device(): jnp.where(joint_index < live_count, coupling[:half_size], 0.0)]
  transfers between devices with their start and end apart: 2 -> 1, of which waited for: 0 -> 0; matrix products, arithmetic and copies ran while one was open for 2% -> 0% of each run, Pallas kernels for 6% -> 5%
where the time goes in v2:
time: 93.1 us; the launch traced here: 92.5 us
  blocking collectives  65.8 us (71%)
  Pallas kernels  26.6 us (29%)
    all_to_all x1, blocking collectives, per_device(): lax.all_to_all(children.reshape(groups, band, width), 'col', split_axis=0...  39.3 us
    all_to_all x1, blocking collectives, per_device(): lax.all_to_all(blocks, ('row', 'col'), split_axis=0, concat_axis=0, axis_...  26.5 us
    pallas_call x1, Pallas kernels, per_device(): pl.pallas_call(merge_kernel, out_shape=jax.ShapeDtypeStruct((2 * groups,...  19.8 us
    pallas_call x1, Pallas kernels, per_device(): pl.pallas_call(prep_kernel, out_shape=(jax.ShapeDtypeStruct((half_size //...  5.05 us
  transfers between devices with their start and end apart: 1, of which 0 were waited for; matrix products, arithmetic and copies ran while one was open for 0% of the time, Pallas kernels for 5%

profile of v2, /device:TPU:0, one launch (start us, length us, event | category | flops | bytes accessed | tf_op | source)
XLA Modules:
  0.0 92.5 jit_solution(17318444738398118308)
XLA Ops:
  0.0 0.0 copy-start
  0.0 0.0 copy-start.1
  0.0 0.0 copy-start.2
  0.0 0.0 copy-start.3
  0.0 0.0 copy-start.4
  0.0 0.0 copy-start.5
  0.0 0.0 copy-start.6
  0.0 39.3 %all_to_all.10.mine = f32[16,96,384]{2,1,0:T(8,128)S(1)} all-to-all(f32[16,96,384]{2,1,0:T(8,128)} %bitcast.16), channel_id=1, replica_groups=mesh['row'=8,'col'=16] {'col'}, dimensions={0} | all-to-all | bytes 4718592 | tf_op jit(solution)/shard_map/all_to_all | solution.py:222
  39.3 0.0 collective-permute-start
  39.4 0.0 copy-done
  39.4 0.0 copy-done.1
  39.4 0.0 copy-done.2
  39.4 0.0 copy-done.3
  39.4 0.0 copy-done.4
  39.4 0.0 copy-done.5
  39.4 0.0 copy-done.6
  39.4 5.1 %shard_map.82 = (f32[48,128]{1,0:T(8,128)S(1)}, f32[6144,128]{1,0:T(8,128)S(1)}, f32[2,2048]{1,0:T(2,128)S(1)}, f32[256,1]{1,0:T(8,128)S(1)}) custom-call(s32[4]{0:T(128)S(1)} %copy-done.6, s32[1]{0:T(128)} %bitcast.core, s32[1]{0:T(128)} %bitcast.2.position, s32[1]{0:T(128)} %bitcast.3.row_index, s32[1]{0:T(128)} %constant.23.clone.1.rows_total, ...), custom_call_target="tpu_custom_call" | custom-call | flops 4000000000 | bytes 4000000 | tf_op jit(solution)/shard_map/pallas_call | solution.py:227
  44.5 0.0 collective-permute-done.other
  44.5 19.8 %shard_map.83 = f32[32,96,128]{2,1,0:T(8,128)S(1)} custom-call(s32[1]{0:T(128)} %bitcast.core, f32[16,96,384]{2,1,0:T(8,128)S(1)} %all_to_all.10.mine, f32[16,96,384]{2,1,0:T(8,128)} %collective-permute-done.other, f32[48,128]{1,0:T(8,128)S(1)} %get-tuple-element.13.column_scale, f32[6144,128]{1,0:T(8,128)S(1)} %get-tuple-element.14.pole_wide, ...), custom_call_target="tpu_custom_call" | custom-call | flops 30000001024 | bytes 10000000 | tf_op jit(solution)/shard_map/pallas_call | solution.py:256
  64.3 26.5 %all_to_all.11.blocks = f32[32,96,128]{2,1,0:T(8,128)S(1)} all-to-all(f32[32,96,128]{2,1,0:T(8,128)S(1)} %shard_map.83), channel_id=1, replica_groups={{0,1,2,3,4,5,6,7,8,9,10,11,12,13,14,15,16,17,18,19,20,21,22,23,24,25,26..., dimensions={0} | all-to-all | bytes 3145728 | tf_op jit(solution)/shard_map/all_to_all | solution.py:271
  90.8 1.7 %shard_map.84 = f32[256,1536]{1,0:T(8,128)} custom-call(f32[32,96,128]{2,1,0:T(8,128)S(1)} %all_to_all.11.blocks, f32[256,1]{1,0:T(8,128)S(1)} %get-tuple-element.16.root_scale), custom_call_target="tpu_custom_call" | custom-call | tf_op jit(solution)/shard_map/pallas_call | solution.py:274
Async XLA Ops:
  0.0 39.4 %copy-start = (s32[12288]{0:T(1024)S(1)}, s32[12288]{0:T(1024)}, u32[]{:S(2)}) copy-start(s32[12288]{0:T(1024)} %param.9) | copy-start | bytes 147460
  0.0 39.4 %copy-start.1 = (f32[12288]{0:T(1024)S(1)}, f32[12288]{0:T(1024)}, u32[]{:S(2)}) copy-start(f32[12288]{0:T(1024)} %param.11) | copy-start | bytes 147460
  0.0 39.4 %copy-start.2 = (f32[12288]{0:T(1024)S(1)}, f32[12288]{0:T(1024)}, u32[]{:S(2)}) copy-start(f32[12288]{0:T(1024)} %param.12) | copy-start | bytes 147460
  0.0 39.4 %copy-start.3 = (f32[12288]{0:T(1024)S(1)}, f32[12288]{0:T(1024)}, u32[]{:S(2)}) copy-start(f32[12288]{0:T(1024)} %param.13) | copy-start | bytes 147460
  0.0 39.4 %copy-start.4 = (s32[4096]{0:T(1024)S(1)}, s32[4096]{0:T(1024)}, u32[]{:S(2)}) copy-start(s32[4096]{0:T(1024)} %param.14) | copy-start | bytes 49156
  0.0 39.4 %copy-start.5 = (f32[4096]{0:T(1024)S(1)}, f32[4096]{0:T(1024)}, u32[]{:S(2)}) copy-start(f32[4096]{0:T(1024)} %param.15) | copy-start | bytes 49156
  0.0 39.4 %copy-start.6 = (s32[4]{0:T(128)S(1)}, s32[4]{0:T(128)}, u32[]{:S(2)}) copy-start(s32[4]{0:T(128)} %counts.1) | copy-start | bytes 52
  39.3 5.1 %collective-permute-start = (f32[16,96,384]{2,1,0:T(8,128)S(1)}, f32[16,96,384]{2,1,0:T(8,128)}, u32[]{:S(2)}, u32[]{:S(2)}) collective-permute-start(f32[16,96,384]{2,1,0:T(8,128)S(1)} %all_to_all.10.mine), channel_id=1, source_target_pairs={{0,16},{16,0},{32,48},{48,32},{64,80},{80,64},{96,112},{112,96},{1... | collective-permute-start | bytes 7077896 | tf_op jit(solution)/shard_map/ppermute | solution.py:226

commit v3 on v2

--- a/solution.py
+++ b/solution.py
@@ -9,7 +9,7 @@
 
 EPSILON = 1e-06
 LANES = 128
-CHUNK = 1024
+CHUNK = 256
 ROOT_TILE = 512
 F32 = jnp.float32
 BF16 = jnp.bfloat16
@@ -42,42 +42,49 @@
 
 def prep_kernel(
     counts, core, position, row_index, rows_total, permutation, rotation, pole_values, coupling,
-    root_gap, root_offset, column_scale, pole_wide, rows, root_scale, gap_mine, table,
+    root_gap, root_offset, column_scale, pole_wide, rows, root_scale, coupling_live, packed,
+    packed_row, place_row, gaps,
 ):
-    live = permutation.shape[1] // 2
+    groups = permutation.shape[0] // 2
+    live = groups * LANES
     share = root_scale.shape[0]
-    blocks = root_gap.shape[1] // share
-    joint = lax.broadcasted_iota(jnp.int32, (1, live), 1)
+    parts = share // LANES
+    shape = (groups, LANES)
+    joint = lax.broadcasted_iota(jnp.int32, shape, 0) * LANES + lax.broadcasted_iota(
+        jnp.int32, shape, 1
+    )
     upper_end = counts[0]
     dense_end = upper_end + counts[1]
     live_count = dense_end + counts[2]
     paired = (joint >= upper_end) & (joint < dense_end)
     lower_only = (joint >= dense_end) & (joint < live_count)
-    angle = rotation[:, :live]
+    angle = rotation[:groups]
     upper_part = jnp.where(joint < upper_end, 1.0, jnp.where(paired, jnp.cos(angle), 0.0))
     lower_part = jnp.where(paired, jnp.sin(angle), jnp.where(lower_only, 1.0, 0.0))
-    upper_used = jnp.where(joint < dense_end, 1.0, 0.0)
-    lower_used = jnp.where(paired | lower_only, 1.0, 0.0)
+    upper_used = jnp.where(joint < dense_end, 1, 0)
+    lower_used = jnp.where(paired | lower_only, 1, 0)
     is_upper = row_index[0] < rows_total[0] // 2
     factor = jnp.where(is_upper, upper_part, lower_part)
     used = jnp.where(is_upper, upper_used, lower_used)
-    coupling_row = jnp.where(joint < live_count, coupling[:, :live], 0.0)
-    pole_row = pole_values[:, :live]
-    order = permutation[:, :live]
+    coupling_live[...] = jnp.where(joint < live_count, coupling[:groups], 0.0)
+    order = permutation[:groups]
     place = jnp.where(order >= live, order - live, order)
-    groups = live // LANES
-    high_place = place // LANES
-    low_place = place - high_place * LANES
-    row_hit = (
-        lax.broadcasted_iota(jnp.int32, (groups, live), 0) == high_place
-    ) & (used > 0.0)
+    packed_place = jnp.where(used > 0, place, -1)
+    values = [*split_three(pole_values[:groups]), *split_three(coupling_live[...] * factor)]
+    for index, piece in enumerate(values):
+        packed[index] = piece.astype(F32)
+    for group in range(groups):
+        here = slice(group * LANES, (group + 1) * LANES)
+        place_row[:, here] = packed_place[group : group + 1, :]
+        for index in range(len(values)):
+            packed_row[index : index + 1, here] = packed[index, group : group + 1, :]
+    row_hit = lax.broadcasted_iota(jnp.int32, (groups, live), 0) == (place_row[...] >> 7)
     low_hit = jnp.where(
-        lax.broadcasted_iota(jnp.int32, (LANES, live), 0) == low_place, 1.0, 0.0
+        lax.broadcasted_iota(jnp.int32, (LANES, live), 0) == (place_row[...] & 127), 1.0, 0.0
     ).astype(BF16)
     pieces = [
-        jnp.where(row_hit, piece.astype(F32), 0.0).astype(BF16)
-        for values in (pole_row, coupling_row * factor)
-        for piece in split_three(values)
+        jnp.where(row_hit, packed_row[index : index + 1, :], 0.0).astype(BF16)
+        for index in range(len(values))
     ]
     spread = product_lanes(jnp.concatenate(pieces, axis=0), low_hit)
     placed = [
@@ -90,56 +97,62 @@
         pole_wide[group * LANES : (group + 1) * LANES, :] = jnp.broadcast_to(
             placed[0][group : group + 1, :], (LANES, LANES)
         ).T
-    table[...] = jnp.zeros_like(table)
-    for group in range(groups):
-        table[group : group + 1, :] = pole_row[:, group * LANES : (group + 1) * LANES]
-    table_pieces = split_three(table[...].T)
-
-    def look_up(index_row):
-        count = index_row.shape[1]
-        high_index = index_row // LANES
-        low_index = index_row - high_index * LANES
-        hit = jnp.where(
-            lax.broadcasted_iota(jnp.int32, (LANES, count), 0) == high_index, 1.0, 0.0
-        ).astype(BF16)
-        total = None
-        for piece in table_pieces:
-            part = product(piece, hit)
-            total = part if total is None else total + part
-        chosen = lax.broadcasted_iota(jnp.int32, (LANES, count), 0) == low_index
-        return jnp.sum(jnp.where(chosen, total, 0.0), axis=0, keepdims=True)
-
-    half_share = share // 2
+
+    blocks = root_gap.shape[0] // parts
+    mine = blocks * LANES
     for block in range(blocks):
-        lanes = pl.ds(pl.multiple_of(block * share + core[0] * half_share, LANES), half_share)
-        here = slice(block * half_share, (block + 1) * half_share)
-        gap_mine[:, here] = root_gap[:, lanes]
-        rows[1:2, here] = root_offset[:, lanes]
-    rows[0:1, :] = look_up(gap_mine[...])
-    own = pl.ds(pl.multiple_of(position[0] * share, LANES), share)
-    base_own = look_up(root_gap[:, own])
-    offset_own = root_offset[:, own]
-    for part in range(share // LANES):
-        lanes = slice(part * LANES, (part + 1) * LANES)
-        base_tall = jnp.broadcast_to(base_own[:, lanes], (LANES, LANES)).T
-        offset_tall = jnp.broadcast_to(offset_own[:, lanes], (LANES, LANES)).T
+        here = slice(block * LANES, (block + 1) * LANES)
+        row = pl.ds(block * parts + core[0], 1)
+        gaps[:, here] = root_gap[row, :]
+        rows[1:2, here] = root_offset[row, :]
+    for part in range(parts):
+        here = slice(mine + part * LANES, mine + (part + 1) * LANES)
+        gaps[:, here] = root_gap[pl.ds(position[0] * parts + part, 1), :]
+    count = gaps.shape[1]
+    hit = jnp.where(
+        lax.broadcasted_iota(jnp.int32, (groups, count), 0) == (gaps[...] >> 7), 1.0, 0.0
+    ).astype(BF16)
+    near = None
+    for piece in split_three(pole_values[:groups]):
+        part = lax.dot_general(
+            piece, hit, (((0,), (0,)), ((), ())), preferred_element_type=F32
+        )
+        near = part if near is None else near + part
+    chosen = lax.broadcasted_iota(jnp.int32, (LANES, count), 0) == (gaps[...] & 127)
+    base = jnp.sum(jnp.where(chosen, near, 0.0), axis=0, keepdims=True)
+    rows[0:1, :] = base[:, :mine]
+    for part in range(parts):
+        lanes = slice(mine + part * LANES, mine + (part + 1) * LANES)
+        base_tall = jnp.broadcast_to(base[:, lanes], (LANES, LANES)).T
+        offset_tall = jnp.broadcast_to(
+            root_offset[pl.ds(position[0] * parts + part, 1), :], (LANES, LANES)
+        ).T
         total = jnp.zeros((LANES, LANES), F32)
         for group in range(groups):
-            where = slice(group * LANES, (group + 1) * LANES)
-            gap = (pole_row[:, where] - base_tall) - offset_tall
-            entry = coupling_row[:, where] * inverse_of(gap)
+            gap = (pole_values[group : group + 1, :] - base_tall) - offset_tall
+            entry = coupling_live[group : group + 1, :] * inverse_of(gap)
             total = total + entry * entry
-        root_scale[lanes, :] = lax.rsqrt(jnp.sum(total, axis=1, keepdims=True) + EPSILON)
-
-
-def merge_kernel(core, mine, other, column_scale, pole_wide, rows, out, pieces):
+        root_scale[part * LANES : (part + 1) * LANES, :] = lax.rsqrt(
+            jnp.sum(total, axis=1, keepdims=True) + EPSILON
+        )
+
+
+def merge_kernel(core, mine, other, column_scale, pole_wide, rows, out, pieces, held, sems):
     groups, band, width = mine.shape
+    quarter = groups // 4
+    copies = []
+    for index in range(4):
+        block = pl.ds(index * quarter, quarter)
+        copies.append(pltpu.make_async_copy(other.at[block], held.at[block], sems.at[index]))
+        copies[index].start()
     parts = width // LANES
     depth = groups * width
     tiles = rows.shape[1] // ROOT_TILE
     per_tile = ROOT_TILE // LANES
-    for half, ref in enumerate((mine, other)):
+    for half, ref in enumerate((mine, held)):
         for source in range(groups):
+            if half == 1 and source % quarter == 0:
+                copies[source // quarter].wait()
             for part in range(parts):
                 lanes = slice(part * LANES, (part + 1) * LANES)
                 first = source * width + part * LANES
@@ -183,13 +196,22 @@
 def finish_kernel(blocks, root_scale, merged, made, sems):
     sources, band, width = blocks.shape
     groups = sources // 2
+    pieces = sems.shape[1]
+    step = groups // pieces
     copies = []
     for half in range(2):
         rows = pl.ds(half * width, width)
-        tall = blocks[half * groups : (half + 1) * groups].reshape(groups * band, width)
-        made[rows, :] = tall.T * root_scale[rows, :]
-        copies.append(pltpu.make_async_copy(made.at[rows], merged.at[rows], sems.at[half]))
-        copies[half].start()
+        for piece in range(pieces):
+            first = half * groups + piece * step
+            tall = blocks[first : first + step].reshape(step * band, width)
+            lanes = pl.ds(piece * step * band, step * band)
+            made[rows, lanes] = tall.T * root_scale[rows, :]
+            copies.append(
+                pltpu.make_async_copy(
+                    made.at[rows, lanes], merged.at[rows, lanes], sems.at[half, piece]
+                )
+            )
+            copies[-1].start()
     for copy in copies:
         copy.wait()
 
@@ -235,8 +257,11 @@
         in_specs=[pl.BlockSpec(memory_space=pltpu.SMEM)] * 5 + vmem(6),
         out_specs=tuple(vmem(4)),
         scratch_shapes=[
-            pltpu.VMEM((1, root_count // 2), jnp.int32),
-            pltpu.VMEM((LANES, LANES), F32),
+            pltpu.VMEM((half_size // LANES, LANES), F32),
+            pltpu.VMEM((6, half_size // LANES, LANES), F32),
+            pltpu.VMEM((6, half_size), F32),
+            pltpu.VMEM((1, half_size), jnp.int32),
+            pltpu.VMEM((1, root_count // 2 + share), jnp.int32),
         ],
         compiler_params=pltpu.CompilerParams(vmem_limit_bytes=32 * 2**20),
         cost_estimate=pl.CostEstimate(
@@ -249,16 +274,20 @@
         row_index.reshape(1),
         jnp.full((1,), rows, jnp.int32),
         *(
-            value.reshape(1, -1)
+            value.reshape(-1, LANES)
             for value in (permutation, rotation, pole_values, coupling, root_gap, root_offset)
         ),
     )
     blocks = pl.pallas_call(
         merge_kernel,
         out_shape=jax.ShapeDtypeStruct((2 * groups, band, share // 2), F32),
-        in_specs=[pl.BlockSpec(memory_space=pltpu.SMEM)] + vmem(5),
+        in_specs=[pl.BlockSpec(memory_space=pltpu.SMEM)] + vmem(1) + hbm(1) + vmem(3),
         out_specs=vmem(1)[0],
-        scratch_shapes=[pltpu.VMEM((4 * band, groups * width), BF16)],
+        scratch_shapes=[
+            pltpu.VMEM((4 * band, groups * width), BF16),
+            pltpu.VMEM((groups, band, width), F32),
+            pltpu.SemaphoreType.DMA((4,)),
+        ],
         compiler_params=pltpu.CompilerParams(vmem_limit_bytes=32 * 2**20),
         cost_estimate=pl.CostEstimate(
             flops=30 * 10**9, bytes_accessed=10 * 10**6, transcendentals=12 * 10**6
@@ -278,7 +307,7 @@
         out_specs=hbm(1)[0],
         scratch_shapes=[
             pltpu.VMEM((share, groups * band), F32),
-            pltpu.SemaphoreType.DMA((2,)),
+            pltpu.SemaphoreType.DMA((2, 4)),
         ],
         compiler_params=pltpu.CompilerParams(vmem_limit_bytes=16 * 2**20),
     )(blocks, root_scale)

time: 93.1 us -> 90.9 us (0.976)
  Pallas kernels: 26.6 us -> 24.4 us
    pallas_call x1, Pallas kernels: 19.8 us -> 17.8 us  [per_device(): pl.pallas_call(merge_kernel, out_shape=jax.ShapeDtypeStruct((2 * groups,...]
where the time goes in v3:
time: 90.9 us; the launch traced here: 90.3 us
  blocking collectives  65.8 us (72%)
  Pallas kernels  24.4 us (27%)
    all_to_all x1, blocking collectives, per_device(): lax.all_to_all(children.reshape(groups, band, width), 'col', split_axis=0...  39.3 us
    all_to_all x1, blocking collectives, per_device(): lax.all_to_all(blocks, ('row', 'col'), split_axis=0, concat_axis=0, axis_...  26.5 us
    pallas_call x1, Pallas kernels, per_device(): pl.pallas_call(merge_kernel, out_shape=jax.ShapeDtypeStruct((2 * groups,...  17.8 us
    pallas_call x1, Pallas kernels, per_device(): pl.pallas_call(prep_kernel, out_shape=(jax.ShapeDtypeStruct((half_size //...  4.93 us
  transfers between devices with their start and end apart: 1, of which 0 were waited for; matrix products, arithmetic and copies ran while one was open for 0% of the time, Pallas kernels for 5%

profile of v3, /device:TPU:0, one launch (start us, length us, event | category | flops | bytes accessed | tf_op | source)
XLA Modules:
  0.0 90.3 jit_solution(817503052854025565)
XLA Ops:
  0.0 0.0 copy-start
  0.0 0.0 copy-start.1
  0.0 0.0 copy-start.2
  0.0 0.0 copy-start.3
  0.0 0.0 copy-start.4
  0.0 0.0 copy-start.5
  0.0 0.0 copy-start.6
  0.0 39.3 %all_to_all.10.mine = f32[16,96,384]{2,1,0:T(8,128)S(1)} all-to-all(f32[16,96,384]{2,1,0:T(8,128)} %bitcast.16), channel_id=1, replica_groups=mesh['row'=8,'col'=16] {'col'}, dimensions={0} | all-to-all | bytes 4718592 | tf_op jit(solution)/shard_map/all_to_all | solution.py:244
  39.3 0.0 collective-permute-start
  39.4 0.0 copy-done
  39.4 0.0 copy-done.1
  39.4 0.0 copy-done.2
  39.4 0.0 copy-done.3
  39.4 0.0 copy-done.4
  39.4 0.0 copy-done.5
  39.4 0.0 copy-done.6
  39.4 4.9 %shard_map.82 = (f32[48,128]{1,0:T(8,128)S(1)}, f32[6144,128]{1,0:T(8,128)S(1)}, f32[2,2048]{1,0:T(2,128)S(1)}, f32[256,1]{1,0:T(8,128)S(1)}) custom-call(s32[4]{0:T(128)S(1)} %copy-done.6, s32[1]{0:T(128)} %bitcast.core, s32[1]{0:T(128)} %bitcast.2.position, s32[1]{0:T(128)} %bitcast.3.row_index, s32[1]{0:T(128)} %constant.23.clone.1.rows_total, ...), custom_call_target="tpu_custom_call" | custom-call | flops 4000000000 | bytes 4000000 | tf_op jit(solution)/shard_map/pallas_call | solution.py:249
  44.3 0.0 collective-permute-done.other
  44.3 17.8 %shard_map.83 = f32[32,96,128]{2,1,0:T(8,128)S(1)} custom-call(s32[1]{0:T(128)} %bitcast.core, f32[16,96,384]{2,1,0:T(8,128)S(1)} %all_to_all.10.mine, f32[16,96,384]{2,1,0:T(8,128)} %collective-permute-done.other, f32[48,128]{1,0:T(8,128)S(1)} %get-tuple-element.13.column_scale, f32[6144,128]{1,0:T(8,128)S(1)} %get-tuple-element.14.pole_wide, ...), custom_call_target="tpu_custom_call" | custom-call | flops 30000001024 | bytes 10000000 | tf_op jit(solution)/shard_map/pallas_call | solution.py:281
  62.1 26.5 %all_to_all.11.blocks = f32[32,96,128]{2,1,0:T(8,128)S(1)} all-to-all(f32[32,96,128]{2,1,0:T(8,128)S(1)} %shard_map.83), channel_id=1, replica_groups={{0,1,2,3,4,5,6,7,8,9,10,11,12,13,14,15,16,17,18,19,20,21,22,23,24,25,26..., dimensions={0} | all-to-all | bytes 3145728 | tf_op jit(solution)/shard_map/all_to_all | solution.py:300
  88.6 1.7 %shard_map.84 = f32[256,1536]{1,0:T(8,128)} custom-call(f32[32,96,128]{2,1,0:T(8,128)S(1)} %all_to_all.11.blocks, f32[256,1]{1,0:T(8,128)S(1)} %get-tuple-element.16.root_scale), custom_call_target="tpu_custom_call" | custom-call | tf_op jit(solution)/shard_map/pallas_call | solution.py:303
Async XLA Ops:
  0.0 39.4 %copy-start = (s32[12288]{0:T(1024)S(1)}, s32[12288]{0:T(1024)}, u32[]{:S(2)}) copy-start(s32[12288]{0:T(1024)} %param.9) | copy-start | bytes 147460
  0.0 39.4 %copy-start.1 = (f32[12288]{0:T(1024)S(1)}, f32[12288]{0:T(1024)}, u32[]{:S(2)}) copy-start(f32[12288]{0:T(1024)} %param.11) | copy-start | bytes 147460
  0.0 39.4 %copy-start.2 = (f32[12288]{0:T(1024)S(1)}, f32[12288]{0:T(1024)}, u32[]{:S(2)}) copy-start(f32[12288]{0:T(1024)} %param.12) | copy-start | bytes 147460
  0.0 39.4 %copy-start.3 = (f32[12288]{0:T(1024)S(1)}, f32[12288]{0:T(1024)}, u32[]{:S(2)}) copy-start(f32[12288]{0:T(1024)} %param.13) | copy-start | bytes 147460
  0.0 39.4 %copy-start.4 = (s32[4096]{0:T(1024)S(1)}, s32[4096]{0:T(1024)}, u32[]{:S(2)}) copy-start(s32[4096]{0:T(1024)} %param.14) | copy-start | bytes 49156
  0.0 39.4 %copy-start.5 = (f32[4096]{0:T(1024)S(1)}, f32[4096]{0:T(1024)}, u32[]{:S(2)}) copy-start(f32[4096]{0:T(1024)} %param.15) | copy-start | bytes 49156
  0.0 39.4 %copy-start.6 = (s32[4]{0:T(128)S(1)}, s32[4]{0:T(128)}, u32[]{:S(2)}) copy-start(s32[4]{0:T(128)} %counts.1) | copy-start | bytes 52
  39.3 5.0 %collective-permute-start = (f32[16,96,384]{2,1,0:T(8,128)S(1)}, f32[16,96,384]{2,1,0:T(8,128)}, u32[]{:S(2)}, u32[]{:S(2)}) collective-permute-start(f32[16,96,384]{2,1,0:T(8,128)S(1)} %all_to_all.10.mine), channel_id=1, source_target_pairs={{0,16},{16,0},{32,48},{48,32},{64,80},{80,64},{96,112},{112,96},{1... | collective-permute-start | bytes 7077896 | tf_op jit(solution)/shard_map/ppermute | solution.py:248

commit v4 on v3

--- a/solution.py
+++ b/solution.py
@@ -47,8 +47,7 @@
 ):
     groups = permutation.shape[0] // 2
     live = groups * LANES
-    share = root_scale.shape[0]
-    parts = share // LANES
+    parts = root_scale.shape[0]
     shape = (groups, LANES)
     joint = lax.broadcasted_iota(jnp.int32, shape, 0) * LANES + lax.broadcasted_iota(
         jnp.int32, shape, 1
@@ -132,8 +131,8 @@
             gap = (pole_values[group : group + 1, :] - base_tall) - offset_tall
             entry = coupling_live[group : group + 1, :] * inverse_of(gap)
             total = total + entry * entry
-        root_scale[part * LANES : (part + 1) * LANES, :] = lax.rsqrt(
-            jnp.sum(total, axis=1, keepdims=True) + EPSILON
+        root_scale[part : part + 1, :] = lax.rsqrt(
+            jnp.sum(total.T, axis=0, keepdims=True) + EPSILON
         )
 
 
@@ -163,7 +162,7 @@
                 pieces[(2 + half) * band : (3 + half) * band, at] = low
 
     def one_tile(tile, carry):
-        first = pl.multiple_of(tile * ROOT_TILE, ROOT_TILE)
+        first = tile * ROOT_TILE
         base_row = rows[0:1, pl.ds(first, ROOT_TILE)]
         offset_row = rows[1:2, pl.ds(first, ROOT_TILE)]
         total = None
@@ -190,7 +189,8 @@
                 out[block] = total[half * band : (half + 1) * band, lanes]
         return carry
 
-    lax.fori_loop(0, tiles, one_tile, 0)
+    for tile in range(tiles):
+        one_tile(tile, 0)
 
 
 def finish_kernel(blocks, root_scale, merged, made, sems):
@@ -205,7 +205,7 @@
             first = half * groups + piece * step
             tall = blocks[first : first + step].reshape(step * band, width)
             lanes = pl.ds(piece * step * band, step * band)
-            made[rows, lanes] = tall.T * root_scale[rows, :]
+            made[rows, lanes] = (tall * root_scale[half : half + 1, :]).T
             copies.append(
                 pltpu.make_async_copy(
                     made.at[rows, lanes], merged.at[rows, lanes], sems.at[half, piece]
@@ -252,7 +252,7 @@
             jax.ShapeDtypeStruct((half_size // LANES, LANES), F32),
             jax.ShapeDtypeStruct((half_size, LANES), F32),
             jax.ShapeDtypeStruct((2, root_count // 2), F32),
-            jax.ShapeDtypeStruct((share, 1), F32),
+            jax.ShapeDtypeStruct((share // LANES, LANES), F32),
         ),
         in_specs=[pl.BlockSpec(memory_space=pltpu.SMEM)] * 5 + vmem(6),
         out_specs=tuple(vmem(4)),

time: 90.9 us -> 90.4 us (level)
  no operation moved by 1% of the time
where the time goes in v4:
time: 90.4 us; the launch traced here: 89.8 us
  blocking collectives  65.8 us (73%)
  Pallas kernels  23.7 us (26%)
    all_to_all x1, blocking collectives, per_device(): lax.all_to_all(children.reshape(groups, band, width), 'col', split_axis=0...  39.3 us
    all_to_all x1, blocking collectives, per_device(): lax.all_to_all(blocks, ('row', 'col'), split_axis=0, concat_axis=0, axis_...  26.5 us
    pallas_call x1, Pallas kernels, per_device(): pl.pallas_call(merge_kernel, out_shape=jax.ShapeDtypeStruct((2 * groups,...  17.5 us
    pallas_call x1, Pallas kernels, per_device(): pl.pallas_call(prep_kernel, out_shape=(jax.ShapeDtypeStruct((half_size //...  4.92 us
  transfers between devices with their start and end apart: 1, of which 0 were waited for; matrix products, arithmetic and copies ran while one was open for 0% of the time, Pallas kernels for 5%

profile of v4, /device:TPU:0, one launch (start us, length us, event | category | flops | bytes accessed | tf_op | source)
XLA Modules:
  0.0 89.8 jit_solution(1864521303689730318)
XLA Ops:
  0.0 0.0 copy-start
  0.0 0.0 copy-start.1
  0.0 0.0 copy-start.2
  0.0 0.0 copy-start.3
  0.0 0.0 copy-start.4
  0.0 0.0 copy-start.5
  0.0 0.0 copy-start.6
  0.0 39.3 %all_to_all.10.mine = f32[16,96,384]{2,1,0:T(8,128)S(1)} all-to-all(f32[16,96,384]{2,1,0:T(8,128)} %bitcast.16), channel_id=1, replica_groups=mesh['row'=8,'col'=16] {'col'}, dimensions={0} | all-to-all | bytes 4718592 | tf_op jit(solution)/shard_map/all_to_all | solution.py:244
  39.3 0.0 collective-permute-start
  39.4 0.0 copy-done
  39.4 0.0 copy-done.1
  39.4 0.0 copy-done.2
  39.4 0.0 copy-done.3
  39.4 0.0 copy-done.4
  39.4 0.0 copy-done.5
  39.4 0.0 copy-done.6
  39.4 4.9 %shard_map.82 = (f32[48,128]{1,0:T(8,128)S(1)}, f32[6144,128]{1,0:T(8,128)S(1)}, f32[2,2048]{1,0:T(2,128)S(1)}, f32[2,128]{1,0:T(2,128)S(1)}) custom-call(s32[4]{0:T(128)S(1)} %copy-done.6, s32[1]{0:T(128)} %bitcast.core, s32[1]{0:T(128)} %bitcast.2.position, s32[1]{0:T(128)} %bitcast.3.row_index, s32[1]{0:T(128)} %constant.23.clone.1.rows_total, ...), custom_call_target="tpu_custom_call" | custom-call | flops 4000000000 | bytes 4000000 | tf_op jit(solution)/shard_map/pallas_call | solution.py:249
  44.3 0.0 collective-permute-done.other
  44.3 17.5 %shard_map.83 = f32[32,96,128]{2,1,0:T(8,128)S(1)} custom-call(s32[1]{0:T(128)} %bitcast.core, f32[16,96,384]{2,1,0:T(8,128)S(1)} %all_to_all.10.mine, f32[16,96,384]{2,1,0:T(8,128)} %collective-permute-done.other, f32[48,128]{1,0:T(8,128)S(1)} %get-tuple-element.13.column_scale, f32[6144,128]{1,0:T(8,128)S(1)} %get-tuple-element.14.pole_wide, ...), custom_call_target="tpu_custom_call" | custom-call | flops 30000001024 | bytes 10000000 | tf_op jit(solution)/shard_map/pallas_call | solution.py:281
  61.8 26.5 %all_to_all.11.blocks = f32[32,96,128]{2,1,0:T(8,128)S(1)} all-to-all(f32[32,96,128]{2,1,0:T(8,128)S(1)} %shard_map.83), channel_id=1, replica_groups={{0,1,2,3,4,5,6,7,8,9,10,11,12,13,14,15,16,17,18,19,20,21,22,23,24,25,26..., dimensions={0} | all-to-all | bytes 3145728 | tf_op jit(solution)/shard_map/all_to_all | solution.py:300
  88.3 1.3 %shard_map.84 = f32[256,1536]{1,0:T(8,128)} custom-call(f32[32,96,128]{2,1,0:T(8,128)S(1)} %all_to_all.11.blocks, f32[2,128]{1,0:T(2,128)S(1)} %get-tuple-element.16.root_scale), custom_call_target="tpu_custom_call" | custom-call | tf_op jit(solution)/shard_map/pallas_call | solution.py:303
Async XLA Ops:
  0.0 39.4 %copy-start = (s32[12288]{0:T(1024)S(1)}, s32[12288]{0:T(1024)}, u32[]{:S(2)}) copy-start(s32[12288]{0:T(1024)} %param.9) | copy-start | bytes 147460
  0.0 39.4 %copy-start.1 = (f32[12288]{0:T(1024)S(1)}, f32[12288]{0:T(1024)}, u32[]{:S(2)}) copy-start(f32[12288]{0:T(1024)} %param.11) | copy-start | bytes 147460
  0.0 39.4 %copy-start.2 = (f32[12288]{0:T(1024)S(1)}, f32[12288]{0:T(1024)}, u32[]{:S(2)}) copy-start(f32[12288]{0:T(1024)} %param.12) | copy-start | bytes 147460
  0.0 39.4 %copy-start.3 = (f32[12288]{0:T(1024)S(1)}, f32[12288]{0:T(1024)}, u32[]{:S(2)}) copy-start(f32[12288]{0:T(1024)} %param.13) | copy-start | bytes 147460
  0.0 39.4 %copy-start.4 = (s32[4096]{0:T(1024)S(1)}, s32[4096]{0:T(1024)}, u32[]{:S(2)}) copy-start(s32[4096]{0:T(1024)} %param.14) | copy-start | bytes 49156
  0.0 39.4 %copy-start.5 = (f32[4096]{0:T(1024)S(1)}, f32[4096]{0:T(1024)}, u32[]{:S(2)}) copy-start(f32[4096]{0:T(1024)} %param.15) | copy-start | bytes 49156
  0.0 39.4 %copy-start.6 = (s32[4]{0:T(128)S(1)}, s32[4]{0:T(128)}, u32[]{:S(2)}) copy-start(s32[4]{0:T(128)} %counts.1) | copy-start | bytes 52
  39.3 5.0 %collective-permute-start = (f32[16,96,384]{2,1,0:T(8,128)S(1)}, f32[16,96,384]{2,1,0:T(8,128)}, u32[]{:S(2)}, u32[]{:S(2)}) collective-permute-start(f32[16,96,384]{2,1,0:T(8,128)S(1)} %all_to_all.10.mine), channel_id=1, source_target_pairs={{0,16},{16,0},{32,48},{48,32},{64,80},{80,64},{96,112},{112,96},{1... | collective-permute-start | bytes 7077896 | tf_op jit(solution)/shard_map/ppermute | solution.py:248

commit v5 on v4

--- a/solution.py
+++ b/solution.py
@@ -47,7 +47,7 @@
 ):
     groups = permutation.shape[0] // 2
     live = groups * LANES
-    parts = root_scale.shape[0]
+    parts = 2
     shape = (groups, LANES)
     joint = lax.broadcasted_iota(jnp.int32, shape, 0) * LANES + lax.broadcasted_iota(
         jnp.int32, shape, 1
@@ -104,9 +104,8 @@
         row = pl.ds(block * parts + core[0], 1)
         gaps[:, here] = root_gap[row, :]
         rows[1:2, here] = root_offset[row, :]
-    for part in range(parts):
-        here = slice(mine + part * LANES, mine + (part + 1) * LANES)
-        gaps[:, here] = root_gap[pl.ds(position[0] * parts + part, 1), :]
+    own_row = pl.ds(position[0] * parts + core[0], 1)
+    gaps[:, mine : mine + LANES] = root_gap[own_row, :]
     count = gaps.shape[1]
     hit = jnp.where(
         lax.broadcasted_iota(jnp.int32, (groups, count), 0) == (gaps[...] >> 7), 1.0, 0.0
@@ -120,20 +119,14 @@
     chosen = lax.broadcasted_iota(jnp.int32, (LANES, count), 0) == (gaps[...] & 127)
     base = jnp.sum(jnp.where(chosen, near, 0.0), axis=0, keepdims=True)
     rows[0:1, :] = base[:, :mine]
-    for part in range(parts):
-        lanes = slice(mine + part * LANES, mine + (part + 1) * LANES)
-        base_tall = jnp.broadcast_to(base[:, lanes], (LANES, LANES)).T
-        offset_tall = jnp.broadcast_to(
-            root_offset[pl.ds(position[0] * parts + part, 1), :], (LANES, LANES)
-        ).T
-        total = jnp.zeros((LANES, LANES), F32)
-        for group in range(groups):
-            gap = (pole_values[group : group + 1, :] - base_tall) - offset_tall
-            entry = coupling_live[group : group + 1, :] * inverse_of(gap)
-            total = total + entry * entry
-        root_scale[part : part + 1, :] = lax.rsqrt(
-            jnp.sum(total.T, axis=0, keepdims=True) + EPSILON
-        )
+    base_tall = jnp.broadcast_to(base[:, mine : mine + LANES], (LANES, LANES)).T
+    offset_tall = jnp.broadcast_to(root_offset[own_row, :], (LANES, LANES)).T
+    total = jnp.zeros((LANES, LANES), F32)
+    for group in range(groups):
+        gap = (pole_values[group : group + 1, :] - base_tall) - offset_tall
+        entry = coupling_live[group : group + 1, :] * inverse_of(gap)
+        total = total + entry * entry
+    root_scale[...] = lax.rsqrt(jnp.sum(total.T, axis=0, keepdims=True) + EPSILON)
 
 
 def merge_kernel(core, mine, other, column_scale, pole_wide, rows, out, pieces, held, sems):
@@ -193,7 +186,7 @@
         one_tile(tile, 0)
 
 
-def finish_kernel(blocks, root_scale, merged, made, sems):
+def finish_kernel(core, blocks, scale_mine, scale_other, merged, made, sems):
     sources, band, width = blocks.shape
     groups = sources // 2
     pieces = sems.shape[1]
@@ -201,11 +194,12 @@
     copies = []
     for half in range(2):
         rows = pl.ds(half * width, width)
+        scale = jnp.where(core[0] == half, scale_mine[...], scale_other[...])
         for piece in range(pieces):
             first = half * groups + piece * step
             tall = blocks[first : first + step].reshape(step * band, width)
             lanes = pl.ds(piece * step * band, step * band)
-            made[rows, lanes] = (tall * root_scale[half : half + 1, :]).T
+            made[rows, lanes] = (tall * scale).T
             copies.append(
                 pltpu.make_async_copy(
                     made.at[rows, lanes], merged.at[rows, lanes], sems.at[half, piece]
@@ -252,7 +246,7 @@
             jax.ShapeDtypeStruct((half_size // LANES, LANES), F32),
             jax.ShapeDtypeStruct((half_size, LANES), F32),
             jax.ShapeDtypeStruct((2, root_count // 2), F32),
-            jax.ShapeDtypeStruct((share // LANES, LANES), F32),
+            jax.ShapeDtypeStruct((1, LANES), F32),
         ),
         in_specs=[pl.BlockSpec(memory_space=pltpu.SMEM)] * 5 + vmem(6),
         out_specs=tuple(vmem(4)),
@@ -261,7 +255,7 @@
             pltpu.VMEM((6, half_size // LANES, LANES), F32),
             pltpu.VMEM((6, half_size), F32),
             pltpu.VMEM((1, half_size), jnp.int32),
-            pltpu.VMEM((1, root_count // 2 + share), jnp.int32),
+            pltpu.VMEM((1, root_count // 2 + LANES), jnp.int32),
         ],
         compiler_params=pltpu.CompilerParams(vmem_limit_bytes=32 * 2**20),
         cost_estimate=pl.CostEstimate(
@@ -278,6 +272,7 @@
             for value in (permutation, rotation, pole_values, coupling, root_gap, root_offset)
         ),
     )
+    other_scale = lax.ppermute(root_scale, "row", pairs)
     blocks = pl.pallas_call(
         merge_kernel,
         out_shape=jax.ShapeDtypeStruct((2 * groups, band, share // 2), F32),
@@ -293,6 +288,7 @@
             flops=30 * 10**9, bytes_accessed=10 * 10**6, transcendentals=12 * 10**6
         ),
     )(core.reshape(1), mine, other, column_scale, pole_wide, root_rows)
+    blocks, other_scale = lax.optimization_barrier((blocks, other_scale))
     chips = [
         [(pair * 2 + half) * groups + index for half in range(2) for index in range(groups)]
         for pair in range(rows // 2)
@@ -303,14 +299,14 @@
     return pl.pallas_call(
         finish_kernel,
         out_shape=jax.ShapeDtypeStruct((share, groups * band), F32),
-        in_specs=vmem(2),
+        in_specs=[pl.BlockSpec(memory_space=pltpu.SMEM)] + vmem(3),
         out_specs=hbm(1)[0],
         scratch_shapes=[
             pltpu.VMEM((share, groups * band), F32),
             pltpu.SemaphoreType.DMA((2, 4)),
         ],
         compiler_params=pltpu.CompilerParams(vmem_limit_bytes=16 * 2**20),
-    )(blocks, root_scale)
+    )(core.reshape(1), blocks, root_scale, other_scale)
 
 
 def solution(mesh):

time: 90.4 us -> 90 us (level)
  Pallas kernels: 23.7 us -> 22.7 us
    pallas_call x1, Pallas kernels: 4.92 us -> 3.89 us  [per_device(): pl.pallas_call(prep_kernel, out_shape=(jax.ShapeDtypeStruct((half_size //...]
  transfers between devices with their start and end apart: 1 -> 2, of which waited for: 0 -> 0; matrix products, arithmetic and copies ran while one was open for 0% -> 0% of each run, Pallas kernels for 5% -> 24%
where the time goes in v5:
time: 90 us; the launch traced here: 89.5 us
  blocking collectives  65.7 us (73%)
  Pallas kernels  22.7 us (25%)
    all_to_all x1, blocking collectives, per_device(): lax.all_to_all(children.reshape(groups, band, width), 'col', split_axis=0...  39.3 us
    all_to_all x1, blocking collectives, per_device(): lax.all_to_all(blocks, ('row', 'col'), split_axis=0, concat_axis=0, axis_...  26.4 us
    pallas_call x1, Pallas kernels, per_device(): pl.pallas_call(merge_kernel, out_shape=jax.ShapeDtypeStruct((2 * groups,...  17.5 us
    pallas_call x1, Pallas kernels, per_device(): pl.pallas_call(prep_kernel, out_shape=(jax.ShapeDtypeStruct((half_size //...  3.89 us
  transfers between devices with their start and end apart: 2, of which 0 were waited for; matrix products, arithmetic and copies ran while one was open for 0% of the time, Pallas kernels for 24%

profile of v5, /device:TPU:0, one launch (start us, length us, event | category | flops | bytes accessed | tf_op | source)
XLA Modules:
  0.0 89.5 jit_solution(10220789097991026503)
XLA Ops:
  0.0 0.0 copy-start
  0.0 0.0 copy-start.1
  0.0 0.0 copy-start.2
  0.0 0.0 copy-start.3
  0.0 0.0 copy-start.4
  0.0 0.0 copy-start.5
  0.0 0.0 copy-start.6
  0.0 39.3 %all_to_all.10.mine = f32[16,96,384]{2,1,0:T(8,128)S(1)} all-to-all(f32[16,96,384]{2,1,0:T(8,128)} %bitcast.16), channel_id=1, replica_groups=mesh['row'=8,'col'=16] {'col'}, dimensions={0} | all-to-all | bytes 4718592 | tf_op jit(solution)/shard_map/all_to_all | solution.py:238
  39.3 0.0 collective-permute-start
  39.4 0.0 copy-done
  39.4 0.0 copy-done.1
  39.4 0.0 copy-done.2
  39.4 0.0 copy-done.3
  39.4 0.0 copy-done.4
  39.4 0.0 copy-done.5
  39.4 0.0 copy-done.6
  39.4 3.9 %shard_map.82 = (f32[48,128]{1,0:T(8,128)S(1)}, f32[6144,128]{1,0:T(8,128)S(1)}, f32[2,2048]{1,0:T(2,128)S(1)}, f32[1,128]{1,0:T(1,128)S(1)}) custom-call(s32[4]{0:T(128)S(1)} %copy-done.6, s32[1]{0:T(128)} %bitcast.core, s32[1]{0:T(128)} %bitcast.2.position, s32[1]{0:T(128)} %bitcast.3.row_index, s32[1]{0:T(128)} %constant.23.clone.1.rows_total, ...), custom_call_target="tpu_custom_call" | custom-call | flops 4000000000 | bytes 4000000 | tf_op jit(solution)/shard_map/pallas_call | solution.py:243
  43.3 0.8 collective-permute-start.1
  44.1 0.0 collective-permute-done.other
  44.1 17.5 %shard_map.83 = f32[32,96,128]{2,1,0:T(8,128)S(1)} custom-call(s32[1]{0:T(128)} %bitcast.core, f32[16,96,384]{2,1,0:T(8,128)S(1)} %all_to_all.10.mine, f32[16,96,384]{2,1,0:T(8,128)} %collective-permute-done.other, f32[48,128]{1,0:T(8,128)S(1)} %get-tuple-element.15.column_scale, f32[6144,128]{1,0:T(8,128)S(1)} %get-tuple-element.16.pole_wide, ...), custom_call_target="tpu_custom_call" | custom-call | flops 30000001024 | bytes 10000000 | tf_op jit(solution)/shard_map/pallas_call | solution.py:276
  61.5 0.0 collective-permute-done.1.scale_other
  61.5 26.4 %all_to_all.11.blocks = f32[32,96,128]{2,1,0:T(8,128)S(1)} all-to-all(f32[32,96,128]{2,1,0:T(8,128)S(1)} %shard_map.83), channel_id=1, replica_groups={{0,1,2,3,4,5,6,7,8,9,10,11,12,13,14,15,16,17,18,19,20,21,22,23,24,25,26..., dimensions={0} | all-to-all | bytes 3145728 | tf_op jit(solution)/shard_map/all_to_all | solution.py:296
  87.9 1.3 %shard_map.84 = f32[256,1536]{1,0:T(8,128)} custom-call(s32[1]{0:T(128)} %bitcast.core, f32[32,96,128]{2,1,0:T(8,128)S(1)} %all_to_all.11.blocks, f32[1,128]{1,0:T(1,128)S(1)} %get-tuple-element.18.scale_mine, f32[1,128]{1,0:T(1,128)S(1)} %collective-permute-done.1.scale_other), custom_call_target="tpu_custom_call" | custom-call | tf_op jit(solution)/shard_map/pallas_call | solution.py:299
Async XLA Ops:
  0.0 39.4 %copy-start = (s32[12288]{0:T(1024)S(1)}, s32[12288]{0:T(1024)}, u32[]{:S(2)}) copy-start(s32[12288]{0:T(1024)} %param.9) | copy-start | bytes 147460
  0.0 39.4 %copy-start.1 = (f32[12288]{0:T(1024)S(1)}, f32[12288]{0:T(1024)}, u32[]{:S(2)}) copy-start(f32[12288]{0:T(1024)} %param.11) | copy-start | bytes 147460
  0.0 39.4 %copy-start.2 = (f32[12288]{0:T(1024)S(1)}, f32[12288]{0:T(1024)}, u32[]{:S(2)}) copy-start(f32[12288]{0:T(1024)} %param.12) | copy-start | bytes 147460
  0.0 39.4 %copy-start.3 = (f32[12288]{0:T(1024)S(1)}, f32[12288]{0:T(1024)}, u32[]{:S(2)}) copy-start(f32[12288]{0:T(1024)} %param.13) | copy-start | bytes 147460
  0.0 39.4 %copy-start.4 = (s32[4096]{0:T(1024)S(1)}, s32[4096]{0:T(1024)}, u32[]{:S(2)}) copy-start(s32[4096]{0:T(1024)} %param.14) | copy-start | bytes 49156
  0.0 39.4 %copy-start.5 = (f32[4096]{0:T(1024)S(1)}, f32[4096]{0:T(1024)}, u32[]{:S(2)}) copy-start(f32[4096]{0:T(1024)} %param.15) | copy-start | bytes 49156
  0.0 39.4 %copy-start.6 = (s32[4]{0:T(128)S(1)}, s32[4]{0:T(128)}, u32[]{:S(2)}) copy-start(s32[4]{0:T(128)} %counts.1) | copy-start | bytes 52
  39.3 4.7 %collective-permute-start = (f32[16,96,384]{2,1,0:T(8,128)S(1)}, f32[16,96,384]{2,1,0:T(8,128)}, u32[]{:S(2)}, u32[]{:S(2)}) collective-permute-start(f32[16,96,384]{2,1,0:T(8,128)S(1)} %all_to_all.10.mine), channel_id=1, source_target_pairs={{0,16},{16,0},{32,48},{48,32},{64,80},{80,64},{96,112},{112,96},{1... | collective-permute-start | bytes 7077896 | tf_op jit(solution)/shard_map/ppermute | solution.py:242
  43.3 18.2 %collective-permute-start.1 = (f32[1,128]{1,0:T(1,128)S(1)}, f32[1,128]{1,0:T(1,128)S(1)}, u32[]{:S(2)}, u32[]{:S(2)}) collective-permute-start(f32[1,128]{1,0:T(1,128)S(1)} %get-tuple-element.18.scale_mine), channel_id=1, source_target_pairs={{0,16},{16,0},{32,48},{48,32},{64,80},{80,64},{96,112},{112,96},{1... | collective-permute-start | bytes 1544 | tf_op jit(solution)/shard_map/ppermute | solution.py:275
